TPU v7x, 32 devices: a whole 2x2x4 slice. The times are simulated.
32 devices in a mesh: tm: 8 (over y, x, core), tile: 4 (over z).
Axes of the slice: x: 2, y: 2, z: 4, core: 2. Of those that a mesh axis runs over, the one named last changes fastest.
Arguments:
- queries: bfloat16 [4096, 1536], P(('tm', 'tile')), may hold values from -16 to 16
- keys: bfloat16 [4096, 1536], P(('tm', 'tile')), may hold values from -16 to 16
- values: bfloat16 [4096, 1536], P(('tm', 'tile')), may hold values from -6 to 6
- grad_out: bfloat16 [4096, 1536], P(('tm', 'tile')), may hold values from -6 to 6
- span_of_group: int32 [8], replicated, may hold values from 0 to 7, each once
- noise_level: int32 [8], replicated, may hold values from 0 to 999
- next_live: int32 [32], replicated, may hold values 0 or 1
- level_bias: float32 [1000, 12], replicated, may hold values from -2 to 2
Outputs:
- attended: bfloat16 [4096, 1536], P(('tm', 'tile'))
- grad_queries: bfloat16 [4096, 1536], P(('tm', 'tile'))
- grad_keys: bfloat16 [4096, 1536], P(('tm', 'tile'))
- grad_values: bfloat16 [4096, 1536], P(('tm', 'tile'))
Inputs may be any that keep to these rules, and one draw needn't show every extreme that they name: span_of_group is a permutation of 0 to 7.
All inputs are finite; a program needn't handle non-finite values.
Results may differ from a plain program's by a relative error of at most 0.019.
Values may be sent and summed in bfloat16 or wider, within the bound.
No kernel may reach another device: no remote copies, remote signals or barrier semaphores. Data moves between devices by JAX's collectives and lax.ppermute only.
A program may use at most 256 MiB of HBM per device.

v0:
```python
import math

import jax
import jax.numpy as jnp
from jax import lax
from jax.sharding import PartitionSpec as P


def shifted(value, axis, by):
    count = lax.axis_size(axis)
    return lax.ppermute(value, axis, [(i, (i + by) % count) for i in range(count)])


def pick_entry(table, index):
    spots = jnp.arange(table.shape[0], dtype=jnp.int32)
    return jnp.sum(jnp.where(spots == index, table, 0), axis=0)


def per_device(queries, keys, values, grad_out, span_of_group, noise_level, next_live, level_bias):
    tok_rows, model_width = queries.shape
    head_count = level_bias.shape[1]
    head_width = model_width // head_count
    inv_root = 1.0 / math.sqrt(head_width)
    groups = lax.axis_size("tm")
    tile_count = lax.axis_size("tile")
    my_group = lax.axis_index("tm")
    my_tile = lax.axis_index("tile")
    group_ids = jnp.arange(groups, dtype=jnp.int32)
    own_span = pick_entry(span_of_group, my_group)
    level_of = jnp.sum(
        jnp.where(span_of_group[:, None] == group_ids[None, :], noise_level[None, :], 0), axis=1
    )
    level_ids = jnp.arange(level_bias.shape[0], dtype=jnp.int32)
    level_table = (level_of[:, None] == level_ids[None, :]).astype(jnp.float32)
    group_bias = jnp.dot(
        level_table, level_bias, precision=lax.Precision.HIGHEST, preferred_element_type=jnp.float32
    )
    second_half = jnp.arange(2 * tok_rows, dtype=jnp.int32) >= tok_rows
    first_half = jnp.logical_not(second_half)
    live_table = next_live.reshape(groups, tile_count)
    live_here = pick_entry(next_live, my_group * tile_count + my_tile)
    attend = span_of_group <= own_span
    key_mask = attend[:, None] & (first_half[None, :] | (live_here == 1))
    near_k, near_v = shifted((keys, values), "tile", -1)
    past_k, past_v, ahead_k, ahead_v = (
        lax.all_gather(keys[None], "tm", axis=0, tiled=True),
        lax.all_gather(values[None], "tm", axis=0, tiled=True),
        lax.all_gather(near_k[None], "tm", axis=0, tiled=True),
        lax.all_gather(near_v[None], "tm", axis=0, tiled=True),
    )
    all_keys = jnp.concatenate([past_k, ahead_k], axis=1).reshape(
        groups, 2 * tok_rows, head_count, head_width
    )
    all_values = jnp.concatenate([past_v, ahead_v], axis=1).reshape(
        groups, 2 * tok_rows, head_count, head_width
    )
    query_heads = queries.reshape(tok_rows, head_count, head_width)
    grad_heads = grad_out.reshape(tok_rows, head_count, head_width)
    scores = jnp.einsum("qhe,jkhe->jhqk", query_heads, all_keys, preferred_element_type=jnp.float32)
    scores = scores * inv_root + group_bias[:, :, None, None]
    scores = jnp.where(key_mask[:, None, None, :], scores, -1e30)
    row_peak = jnp.max(scores, axis=(0, 3))
    log_total = row_peak + jnp.log(
        jnp.sum(jnp.exp(scores - row_peak[None, :, :, None]), axis=(0, 3))
    )
    weights_full = jnp.exp(scores - log_total[None, :, :, None])
    weights_low = weights_full.astype(jnp.bfloat16)
    attended = jnp.einsum(
        "jhqk,jkhe->qhe", weights_low, all_values, preferred_element_type=jnp.float32
    ).astype(jnp.bfloat16)
    row_delta = jnp.sum(grad_heads.astype(jnp.float32) * attended.astype(jnp.float32), axis=2).T
    grad_weights = jnp.einsum(
        "qhe,jkhe->jhqk", grad_heads, all_values, preferred_element_type=jnp.float32
    )
    grad_scores = (weights_full * (grad_weights - row_delta[None, :, :, None]) * inv_root).astype(
        jnp.bfloat16
    )
    grad_queries = jnp.einsum(
        "jhqk,jkhe->qhe", grad_scores, all_keys, preferred_element_type=jnp.float32
    )
    grad_queries = grad_queries.astype(jnp.bfloat16).reshape(tok_rows, model_width)
    near_q, near_g = shifted((queries, grad_out), "tile", 1)
    near_lse, near_delta = shifted((log_total, row_delta), "tile", 1)
    past_q, past_g, prev_q, prev_g = (
        lax.all_gather(queries[None], "tm", axis=0, tiled=True),
        lax.all_gather(grad_out[None], "tm", axis=0, tiled=True),
        lax.all_gather(near_q[None], "tm", axis=0, tiled=True),
        lax.all_gather(near_g[None], "tm", axis=0, tiled=True),
    )
    past_lse, past_delta, prev_lse, prev_delta = (
        lax.all_gather(log_total[None], "tm", axis=0, tiled=True),
        lax.all_gather(row_delta[None], "tm", axis=0, tiled=True),
        lax.all_gather(near_lse[None], "tm", axis=0, tiled=True),
        lax.all_gather(near_delta[None], "tm", axis=0, tiled=True),
    )
    source_q = jnp.concatenate([past_q, prev_q], axis=1).reshape(
        groups, 2 * tok_rows, head_count, head_width
    )
    source_g = jnp.concatenate([past_g, prev_g], axis=1).reshape(
        groups, 2 * tok_rows, head_count, head_width
    )
    source_lse = jnp.concatenate([past_lse, prev_lse], axis=2)
    source_delta = jnp.concatenate([past_delta, prev_delta], axis=2)
    prev_tile = (my_tile + tile_count - 1) % tile_count
    tile_ids = jnp.arange(tile_count, dtype=jnp.int32)
    prev_live = jnp.sum(jnp.where(tile_ids[None, :] == prev_tile, live_table, 0), axis=1)
    seen_by = own_span <= span_of_group
    query_mask = seen_by[:, None] & (first_half[None, :] | (prev_live[:, None] == 1))
    my_bias = jnp.sum(jnp.where(group_ids[:, None] == my_group, group_bias, 0.0), axis=0)
    key_heads = keys.reshape(tok_rows, head_count, head_width)
    value_heads = values.reshape(tok_rows, head_count, head_width)
    back_scores = jnp.einsum(
        "gqhe,khe->ghqk", source_q, key_heads, preferred_element_type=jnp.float32
    )
    back_scores = back_scores * inv_root + my_bias[None, :, None, None]
    back_full = jnp.where(
        query_mask[:, None, :, None], jnp.exp(back_scores - source_lse[:, :, :, None]), 0.0
    )
    back_low = back_full.astype(jnp.bfloat16)
    back_grad = jnp.einsum(
        "gqhe,khe->ghqk", source_g, value_heads, preferred_element_type=jnp.float32
    )
    back_ds = (back_full * (back_grad - source_delta[:, :, :, None]) * inv_root).astype(
        jnp.bfloat16
    )
    grad_keys = jnp.einsum("ghqk,gqhe->khe", back_ds, source_q, preferred_element_type=jnp.float32)
    grad_values = jnp.einsum(
        "ghqk,gqhe->khe", back_low, source_g, preferred_element_type=jnp.float32
    )
    grad_keys = grad_keys.astype(jnp.bfloat16).reshape(tok_rows, model_width)
    grad_values = grad_values.astype(jnp.bfloat16).reshape(tok_rows, model_width)
    return (attended.reshape(tok_rows, model_width), grad_queries, grad_keys, grad_values)


def solution(mesh):
    in_specs = (
        P(("tm", "tile"), None),
        P(("tm", "tile"), None),
        P(("tm", "tile"), None),
        P(("tm", "tile"), None),
        P(),
        P(),
        P(),
        P(),
    )
    out_specs = (
        P(("tm", "tile"), None),
        P(("tm", "tile"), None),
        P(("tm", "tile"), None),
        P(("tm", "tile"), None),
    )
    return jax.shard_map(
        per_device, mesh=mesh, in_specs=in_specs, out_specs=out_specs, check_vma=False
    )
```

profile of v0, /device:TPU:0, one launch (start us, length us, event | category | flops | bytes accessed | tf_op | source)
XLA Modules:
  0.0 362.9 jit_solution(2794060304798393513)
XLA Ops:
  13.1 8.7 %collective-permute-done.1 = bf16[128,1536]{1,0:T(8,128)(2,1)S(1)} collective-permute-done((bf16[128,1536]{1,0:T(8,128)(2,1)}, bf16[128,1536]{1,0:T(8,128)(2,1)S(1)}, u32[]{:S(2)}, u32[]{:S(2)}) %collective-permute-start.1) | collective-permute-done | bytes 393248 | tf_op jit(solution)/shard_map/ppermute | solution.py:11
  27.5 7.8 %collective-permute-done = bf16[128,1536]{1,0:T(8,128)(2,1)S(1)} collective-permute-done((bf16[128,1536]{1,0:T(8,128)(2,1)}, bf16[128,1536]{1,0:T(8,128)(2,1)S(1)}, u32[]{:S(2)}, u32[]{:S(2)}) %collective-permute-start) | collective-permute-done | bytes 393248 | tf_op jit(solution)/shard_map/ppermute | solution.py:11
  36.8 11.7 %collective-permute-done.2 = bf16[128,1536]{1,0:T(8,128)(2,1)S(1)} collective-permute-done((bf16[128,1536]{1,0:T(8,128)(2,1)}, bf16[128,1536]{1,0:T(8,128)(2,1)S(1)}, u32[]{:S(2)}, u32[]{:S(2)}) %collective-permute-start.2) | collective-permute-done | bytes 393248 | tf_op jit(solution)/shard_map/ppermute | solution.py:11
  63.4 16.4 %all-gather.31.cloned.1.call-done = bf16[1024,1536]{1,0:T(8,128)(2,1)} async-done(((bf16[128,1536]{1,0:T(8,128)(2,1)}), bf16[1024,1536]{1,0:T(8,128)(2,1)}) %all-gather.31.cloned.1.call-update) | async-done | bytes 3145744 | tf_op jit(solution)/shard_map/all_gather | solution.py:48
  85.6 8.6 %copy.102 = bf16[8,256,1536]{1,2,0:T(8,128)(2,1)} copy(bf16[8,256,1536]{2,1,0:T(8,128)(2,1)} %pad_maximum_fusion.1) | data formatting | bytes 12582912 | tf_op jit(solution)/shard_map/concatenate | solution.py:51
  94.2 8.8 %fusion.26 = (f32[12,128]{1,0:T(8,128)S(1)}, f32[12,8,256,128]{3,2,1,0:T(8,128)}) fusion(f32[8,12]{0,1:T(8,128)S(1)} %copy.106, pred[8,256]{1,0:T(8,128)(4,1)S(1)} %broadcast_and_fusion, bf16[128,12,128,1]{0,2,3,1:T(8,128)(2,1)S(1)} %bitcast.140, bf16[8,256,12,128]{1,3,2,0:T(8,128)(2,1)} %bitcast.118), kind=kOutput, calls=%fused_computation.36 | convolution fusion | flops 817887744 | bytes 19276160 | tf_op jit(solution)/shard_map/qhe,jkhe->jhqk/dot_general | solution.py:59
  103.0 11.0 %all-gather.25.cloned.1.call-done = bf16[1024,1536]{1,0:T(8,128)(2,1)} async-done(((bf16[128,1536]{1,0:T(8,128)(2,1)}), bf16[1024,1536]{1,0:T(8,128)(2,1)}) %all-gather.25.cloned.1.call-update) | async-done | bytes 3145744 | tf_op jit(solution)/shard_map/all_gather | solution.py:47
  114.0 34.7 %all-gather.27.cloned.1.call-done = bf16[1024,1536]{1,0:T(8,128)(2,1)} async-done(((bf16[128,1536]{1,0:T(8,128)(2,1)}), bf16[1024,1536]{1,0:T(8,128)(2,1)}) %all-gather.27.cloned.1.call-update) | async-done | bytes 3145744 | tf_op jit(solution)/shard_map/all_gather | solution.py:49
  154.6 8.6 %copy.101 = bf16[8,256,1536]{1,2,0:T(8,128)(2,1)} copy(bf16[8,256,1536]{2,1,0:T(8,128)(2,1)} %pad_maximum_fusion) | data formatting | bytes 12582912 | tf_op jit(solution)/shard_map/concatenate | solution.py:54
  163.1 7.5 %exponential_reduce_fusion = f32[12,128]{1,0:T(8,128)S(1)} fusion(f32[12,128]{1,0:T(8,128)S(1)} %get-tuple-element.26, f32[8,12]{0,1:T(8,128)S(1)} %copy.106, f32[12,8,256,128]{3,2,1,0:T(8,128)} %get-tuple-element.27, pred[8,256]{1,0:T(8,128)(4,1)S(1)} %broadcast_and_fusion), kind=kLoop, calls=%fused_computation.13 | loop fusion | flops 15727104 | bytes 12597632 | tf_op jit(solution)/shard_map/reduce_sum | solution.py:64
  172.1 10.0 %multiply_reduce_fusion = (f32[128,12]{0,1:T(8,128)S(1)}, bf16[12,128,128]{2,1,0:T(8,128)(2,1)}) fusion(bf16[128,12,128]{0,2,1:T(8,128)(2,1)S(1)} %bitcast.138, bf16[8,256,12,128]{1,3,2,0:T(8,128)(2,1)S(1)} %bitcast.127, f32[12,128]{1,0:T(8,128)S(1)} %log_add_fusion, f32[8,12]{0,1:T(8,128)S(1)} %copy.106, f32[12,8,256,128]{3,2,1,0:T(8,128)} %get-tuple-element.27, ...), kind=kOutput, calls=%fused_computation.45 | convolution fusion | flops 822016512 | bytes 19675520 | tf_op jit(solution)/shard_map/jhqk,jkhe->qhe/dot_general | solution.py:68
  185.5 10.8 %fusion.6 = bf16[8,12,128,256]{2,3,0,1:T(8,128)(2,1)S(1)} fusion(f32[12,128]{1,0:T(8,128)S(1)} %bitcast.147, f32[12,128]{1,0:T(8,128)S(1)} %log_add_fusion, f32[8,12]{0,1:T(8,128)S(1)} %copy.106, f32[12,8,256,128]{3,2,1,0:T(8,128)} %get-tuple-element.27, pred[8,256]{1,0:T(8,128)(4,1)S(1)} %broadcast_and_fusion, bf16[128,12,128,1]{0,2,3,1:T(8,128)(2,1)S(1)} %bitcast.139, ...), kind=kOutput, calls=%fused_computation.9 | convolution fusion | flops 830472192 | bytes 25573760 | tf_op jit(solution)/shard_map/qhe,jkhe->jhqk/dot_general | solution.py:72
  199.1 17.7 %all-gather.35.cloned.1.call-done = bf16[1024,1536]{1,0:T(8,128)(2,1)} async-done(((bf16[128,1536]{1,0:T(8,128)(2,1)}), bf16[1024,1536]{1,0:T(8,128)(2,1)}) %all-gather.35.cloned.1.call-update) | async-done | bytes 3145744 | tf_op jit(solution)/shard_map/all_gather | solution.py:87
  222.7 8.7 %copy.112 = bf16[8,256,1536]{1,2,0:T(8,128)(2,1)} copy(bf16[8,256,1536]{2,1,0:T(8,128)(2,1)} %pad_maximum_fusion.2) | data formatting | bytes 12582912 | tf_op jit(solution)/shard_map/concatenate | solution.py:96
  231.4 9.1 %all-gather.12 = f32[8,12,128]{2,1,0:T(8,128)S(1)} all-gather(f32[1,12,128]{2,1,0:T(8,128)S(1)} %bitcast.145), channel_id=8, replica_groups=mesh['tm'=8,'tile'=4] {'tm'}, dimensions={0}, use_global_device_ids=true | all-gather | bytes 55296 | tf_op jit(solution)/shard_map/all_gather | solution.py:91
  240.5 10.6 %all-gather.37.cloned.1.call-done = bf16[1024,1536]{1,0:T(8,128)(2,1)} async-done(((bf16[128,1536]{1,0:T(8,128)(2,1)}), bf16[1024,1536]{1,0:T(8,128)(2,1)}) %all-gather.37.cloned.1.call-update) | async-done | bytes 3145744 | tf_op jit(solution)/shard_map/all_gather | solution.py:86
  251.1 34.2 %all-gather.39.cloned.1.call-done = bf16[1024,1536]{1,0:T(8,128)(2,1)} async-done(((bf16[128,1536]{1,0:T(8,128)(2,1)}), bf16[1024,1536]{1,0:T(8,128)(2,1)}) %all-gather.39.cloned.1.call-update) | async-done | bytes 3145744 | tf_op jit(solution)/shard_map/all_gather | solution.py:88
  291.2 8.6 %copy.117 = bf16[8,256,1536]{1,2,0:T(8,128)(2,1)} copy(bf16[8,256,1536]{2,1,0:T(8,128)(2,1)} %pad_maximum_fusion.3) | data formatting | bytes 12582912 | tf_op jit(solution)/shard_map/concatenate | solution.py:99
  299.7 9.2 %all-gather.14 = f32[8,12,128]{2,1,0:T(8,128)S(1)} all-gather(f32[1,12,128]{2,1,0:T(8,128)S(1)} %bitcast.148), channel_id=12, replica_groups=mesh['tm'=8,'tile'=4] {'tm'}, dimensions={0}, use_global_device_ids=true | all-gather | bytes 55296 | tf_op jit(solution)/shard_map/all_gather | solution.py:92
  308.9 8.3 %all-gather.13 = f32[8,12,128]{2,1,0:T(8,128)S(1)} all-gather(f32[1,12,128]{2,1,0:T(8,128)S(1)} %bitcast.150), channel_id=9, replica_groups=mesh['tm'=8,'tile'=4] {'tm'}, dimensions={0}, use_global_device_ids=true | all-gather | bytes 55296 | tf_op jit(solution)/shard_map/all_gather | solution.py:93
  317.3 9.7 %all-gather.15 = f32[8,12,128]{2,1,0:T(8,128)S(1)} all-gather(f32[1,12,128]{2,1,0:T(8,128)S(1)} %bitcast.149), channel_id=13, replica_groups=mesh['tm'=8,'tile'=4] {'tm'}, dimensions={0}, use_global_device_ids=true | all-gather | bytes 55296 | tf_op jit(solution)/shard_map/all_gather | solution.py:94
  327.0 9.3 %fusion.9 = (bf16[8,12,256,128]{3,2,0,1:T(8,128)(2,1)}, f32[12,8,256,128]{3,2,1,0:T(8,128)S(1)}) fusion(f32[8,12,256]{2,0,1:T(8,128)S(1)} %copy.116, f32[12]{0:T(128)S(1)} %get-tuple-element.30, pred[8,256]{1,0:T(8,128)(4,1)S(1)} %or_and_fusion, bf16[128,12,128,1]{0,2,3,1:T(8,128)(2,1)S(1)} %bitcast.137, bf16[8,256,12,128]{1,3,2,0:T(8,128)(2,1)} %bitcast.114), kind=kOutput, calls=%fused_computation.15 | convolution fusion | flops 821035008 | bytes 25659440 | tf_op jit(solution)/shard_map/gqhe,khe->ghqk/dot_general | solution.py:112
  336.4 9.6 %fusion.2 = bf16[8,12,256,128]{3,2,0,1:T(8,128)(2,1)S(1)} fusion(f32[12,8,256,128]{3,2,1,0:T(8,128)S(1)} %get-tuple-element.33, f32[8,12,256]{2,0,1:T(8,128)S(1)} %copy.121, f32[8,12,256]{2,0,1:T(8,128)S(1)} %copy.116, f32[12]{0:T(128)S(1)} %get-tuple-element.30, pred[8,256]{1,0:T(8,128)(4,1)S(1)} %or_and_fusion, ...), kind=kOutput, calls=%fused_computation.3 | convolution fusion | flops 830472192 | bytes 25757744 | tf_op jit(solution)/shard_map/gqhe,khe->ghqk/dot_general | solution.py:120
  348.7 6.4 %fusion.49 = bf16[12,128,128]{2,1,0:T(8,128)(2,1)S(1)} fusion(bf16[8,256,12,128]{1,3,2,0:T(8,128)(2,1)} %bitcast.122, bf16[8,12,256,128]{3,2,0,1:T(8,128)(2,1)} %get-tuple-element.32), kind=kOutput, calls=%fused_computation.43 | convolution fusion | flops 805502976 | bytes 12976128 | tf_op jit(solution)/shard_map/ghqk,gqhe->khe/dot_general | solution.py:127
  (92 shorter events, 62.2 us)
Async XLA Ops:
  7.2 49.5 %copy-start = (f32[1000,12]{0,1:T(8,128)S(1)}, f32[1000,12]{0,1:T(8,128)}, u32[]{:S(2)}) copy-start(f32[1000,12]{0,1:T(8,128)} %param.15) | copy-start | bytes 144004
  7.2 56.2 %all-gather.29.cloned.1.call-start = ((), (), s32[]{:S(2)}) async-start(), calls=%async_computation.2 | async-start | bytes 3538944 | tf_op jit(solution)/shard_map/all_gather | solution.py:46
  7.9 71.8 %all-gather.31.cloned.1.call-start = ((), (), s32[]{:S(2)}) async-start(), calls=%async_computation.3 | async-start | bytes 3538944 | tf_op jit(solution)/shard_map/all_gather | solution.py:48
  8.0 13.8 %collective-permute-start.1 = (bf16[128,1536]{1,0:T(8,128)(2,1)}, bf16[128,1536]{1,0:T(8,128)(2,1)S(1)}, u32[]{:S(2)}, u32[]{:S(2)}) collective-permute-start(bf16[128,1536]{1,0:T(8,128)(2,1)} %param.9), channel_id=1, source_target_pairs={{0,3},{1,0},{2,1},{3,2},{4,7},{5,4},{6,5},{7,6},{8,11},{9,8},{10,9... | collective-permute-start | bytes 1179656 | tf_op jit(solution)/shard_map/ppermute | solution.py:11
  22.5 91.5 %all-gather.25.cloned.1.call-start = ((), (), s32[]{:S(2)}) async-start(), calls=%async_computation | async-start | bytes 3538944 | tf_op jit(solution)/shard_map/all_gather | solution.py:47
  23.3 125.4 %all-gather.27.cloned.1.call-start = ((), (), s32[]{:S(2)}) async-start(), calls=%async_computation.1 | async-start | bytes 3538944 | tf_op jit(solution)/shard_map/all_gather | solution.py:49
  23.3 12.0 %collective-permute-start = (bf16[128,1536]{1,0:T(8,128)(2,1)}, bf16[128,1536]{1,0:T(8,128)(2,1)S(1)}, u32[]{:S(2)}, u32[]{:S(2)}) collective-permute-start(bf16[128,1536]{1,0:T(8,128)(2,1)} %param.10), channel_id=1, source_target_pairs={{0,3},{1,0},{2,1},{3,2},{4,7},{5,4},{6,5},{7,6},{8,11},{9,8},{10,9... | collective-permute-start | bytes 1179656 | tf_op jit(solution)/shard_map/ppermute | solution.py:11
  36.1 163.0 %all-gather.33.cloned.1.call-start = ((), (), s32[]{:S(2)}) async-start(), calls=%async_computation.4 | async-start | bytes 3538944 | tf_op jit(solution)/shard_map/all_gather | solution.py:85
  36.7 180.1 %all-gather.35.cloned.1.call-start = ((), (), s32[]{:S(2)}) async-start(), calls=%async_computation.5 | async-start | bytes 3538944 | tf_op jit(solution)/shard_map/all_gather | solution.py:87
  36.8 11.8 %collective-permute-start.2 = (bf16[128,1536]{1,0:T(8,128)(2,1)}, bf16[128,1536]{1,0:T(8,128)(2,1)S(1)}, u32[]{:S(2)}, u32[]{:S(2)}) collective-permute-start(bf16[128,1536]{1,0:T(8,128)(2,1)} %param.8), channel_id=1, source_target_pairs={{0,1},{1,2},{2,3},{3,0},{4,5},{5,6},{6,7},{7,4},{8,9},{9,10},{10,1... | collective-permute-start | bytes 1179656 | tf_op jit(solution)/shard_map/ppermute | solution.py:11
  49.3 201.8 %all-gather.37.cloned.1.call-start = ((), (), s32[]{:S(2)}) async-start(), calls=%async_computation.6 | async-start | bytes 3538944 | tf_op jit(solution)/shard_map/all_gather | solution.py:86
  50.0 235.3 %all-gather.39.cloned.1.call-start = ((), (), s32[]{:S(2)}) async-start(), calls=%async_computation.7 | async-start | bytes 3538944 | tf_op jit(solution)/shard_map/all_gather | solution.py:88
  50.1 12.5 %collective-permute-start.4 = (bf16[128,1536]{1,0:T(8,128)(2,1)}, bf16[128,1536]{1,0:T(8,128)(2,1)S(1)}, u32[]{:S(2)}, u32[]{:S(2)}) collective-permute-start(bf16[128,1536]{1,0:T(8,128)(2,1)} %param.11), channel_id=1, source_target_pairs={{0,1},{1,2},{2,3},{3,0},{4,5},{5,6},{6,7},{7,4},{8,9},{9,10},{10,1... | collective-permute-start | bytes 1179656 | tf_op jit(solution)/shard_map/ppermute | solution.py:11
  163.1 9.0 %copy-start.2 = (bf16[8,256,1536]{1,2,0:T(8,128)(2,1)S(1)}, bf16[8,256,1536]{1,2,0:T(8,128)(2,1)}, u32[]{:S(2)}) copy-start(bf16[8,256,1536]{1,2,0:T(8,128)(2,1)} %copy.101) | copy-start | bytes 18874372
  163.1 9.0 %copy-start.7 = (bf16[128,1536]{0,1:T(8,128)(2,1)S(1)}, bf16[128,1536]{0,1:T(8,128)(2,1)}, u32[]{:S(2)}) copy-start(bf16[128,1536]{0,1:T(8,128)(2,1)} %copy.108) | copy-start | bytes 1179652
  170.6 138.3 %collective-permute-start.3 = (f32[12,128]{1,0:T(8,128)S(1)}, f32[12,128]{1,0:T(8,128)S(1)}, u32[]{:S(2)}, u32[]{:S(2)}) collective-permute-start(f32[12,128]{1,0:T(8,128)S(1)} %log_add_fusion), channel_id=1, source_target_pairs={{0,1},{1,2},{2,3},{3,0},{4,5},{5,6},{6,7},{7,4},{8,9},{9,10},{10,1... | collective-permute-start | bytes 18440 | tf_op jit(solution)/shard_map/ppermute | solution.py:11
  172.1 24.2 %slice-start.2 = ((s8[6291456]{0:T(1024)(128)(4,1)}), s8[2097152]{0:T(1024)(128)(4,1)S(1)}, s32[]{:S(2)}) async-start(s8[6291456]{0:T(1024)(128)(4,1)} %bitcast.119), calls=%async_computation.10 | async-start | bytes 4194304
  184.0 133.2 %collective-permute-start.5 = (f32[12,128]{1,0:T(8,128)S(1)}, f32[12,128]{1,0:T(8,128)S(1)}, u32[]{:S(2)}, u32[]{:S(2)}) collective-permute-start(f32[12,128]{1,0:T(8,128)S(1)} %bitcast.146), channel_id=1, source_target_pairs={{0,1},{1,2},{2,3},{3,0},{4,5},{5,6},{6,7},{7,4},{8,9},{9,10},{10,1... | collective-permute-start | bytes 18440 | tf_op jit(solution)/shard_map/ppermute | solution.py:11
  185.5 10.8 %slice-start.3 = ((s8[6291456]{0:T(1024)(128)(4,1)}), s8[4194304]{0:T(1024)(128)(4,1)S(1)}, s32[]{:S(2)}) async-start(s8[6291456]{0:T(1024)(128)(4,1)} %bitcast.119), calls=%async_computation.11 | async-start | bytes 8388608
  317.2 28.8 %slice-start = ((s8[6291456]{0:T(1024)(128)(4,1)}), s8[4194304]{0:T(1024)(128)(4,1)S(1)}, s32[]{:S(2)}) async-start(s8[6291456]{0:T(1024)(128)(4,1)} %bitcast.115), calls=%async_computation.8 | async-start | bytes 8388608
  326.9 9.5 %slice-start.4 = ((s8[6291456]{0:T(1024)(128)(4,1)}), s8[4194304]{0:T(1024)(128)(4,1)S(1)}, s32[]{:S(2)}) async-start(s8[6291456]{0:T(1024)(128)(4,1)} %bitcast.123), calls=%async_computation.12 | async-start | bytes 8388608
  327.0 9.4 %slice-start.5 = ((s8[6291456]{0:T(1024)(128)(4,1)}), s8[2097152]{0:T(1024)(128)(4,1)S(1)}, s32[]{:S(2)}) async-start(s8[6291456]{0:T(1024)(128)(4,1)} %bitcast.123), calls=%async_computation.13 | async-start | bytes 4194304
  327.0 18.9 %slice-start.1 = ((s8[6291456]{0:T(1024)(128)(4,1)}), s8[2097152]{0:T(1024)(128)(4,1)S(1)}, s32[]{:S(2)}) async-start(s8[6291456]{0:T(1024)(128)(4,1)} %bitcast.115), calls=%async_computation.9 | async-start | bytes 4194304
  348.7 7.4 %copy-start.1 = (f32[1000,12]{0,1:T(8,128)S(1)}, f32[1000,12]{0,1:T(8,128)}, u32[]{:S(2)}) copy-start(f32[1000,12]{0,1:T(8,128)} %param.15) | copy-start | bytes 144004
  (4 other events, 3.0 us)
Sparse Core Ops, SparseCore 0:
  9.9 35.0 all-gather.28
  47.4 32.3 all-gather.30
  81.6 32.3 all-gather.24
  116.3 32.3 all-gather.26
  150.4 32.3 all-gather.32
  184.5 32.3 all-gather.34
  218.7 32.3 all-gather.36
  252.9 32.3 all-gather.38
where the time goes:
time: 364 us; the launch traced here: 363 us
  waiting for transfers between devices  155 us (43%)
  matrix products  58.7 us (16%)
  local copies, waits for them, and re-layouts  48.7 us (13%)
  blocking collectives  36.2 us (10%)
  other arithmetic  36 us (10%)
  between operations  15.1 us (4%)
  starting transfers between devices  12.8 us (4%)
    all_gather x1, waiting for transfers between devices, per_device(): lax.all_gather(near_v[None], 'tm', axis=0, tiled=True)  34.7 us
    all_gather x1, waiting for transfers between devices, per_device(): lax.all_gather(near_g[None], 'tm', axis=0, tiled=True)  34.2 us
    ppermute x6, waiting for transfers between devices, shifted(): lax.ppermute(value, axis, [(i, (i + by) % count) for i in range(count)])  28.2 us
    all_gather x1, waiting for transfers between devices, per_device(): lax.all_gather(near_q[None], 'tm', axis=0, tiled=True)  17.7 us
    all_gather x1, waiting for transfers between devices, per_device(): lax.all_gather(near_k[None], 'tm', axis=0, tiled=True)  16.4 us
    unnamed x36, local copies, waits for them, and re-layouts  13.3 us
    ppermute x6, starting transfers between devices, shifted(): lax.ppermute(value, axis, [(i, (i + by) % count) for i in range(count)])  12.5 us
    all_gather x1, waiting for transfers between devices, per_device(): lax.all_gather(values[None], 'tm', axis=0, tiled=True)  11 us
  transfers between devices with their start and end apart: 14, of which 9 were waited for; matrix products, arithmetic and copies ran while one was open for 31% of the time, Pallas kernels for 0%

commit v1 on v0

v1 whole, which is shorter than its diff:
```python
import functools
import math

import jax
import jax.numpy as jnp
from jax import lax
from jax.experimental import pallas as pl
from jax.experimental.pallas import tpu as pltpu
from jax.sharding import PartitionSpec as P

VMEM = pltpu.VMEM
SMEM = pltpu.SMEM
BF16 = jnp.bfloat16
F32 = jnp.float32
NT = (((1,), (1,)), ((), ()))
LOG2E = 1.4426950408889634


def params(mib):
    return pltpu.CompilerParams(vmem_limit_bytes=mib * 1024 * 1024)


def whole(space):
    return pl.BlockSpec(memory_space=space)


def shard_count(heads, groups):
    count = 1
    while heads % (2 * count) == 0 and groups % (2 * count) == 0:
        count *= 2
    return count


def pack_kernel(shards, width, pos_ref, q_ref, g_ref, k_ref, v_ref, *outs):
    shard = pos_ref[0]
    for hop in range(shards):
        lane = pl.multiple_of((shard ^ hop) * width, 128)
        full, pair = outs[hop], outs[shards + hop]
        full[0] = q_ref[:, pl.ds(lane, width)]
        full[1] = g_ref[:, pl.ds(lane, width)]
        k = k_ref[:, pl.ds(lane, width)]
        v = v_ref[:, pl.ds(lane, width)]
        full[2] = k
        full[3] = v
        pair[0] = k
        pair[1] = v


def attention_kernel(shards, replicas, tiles, inv_root, *refs):
    groups = shards * replicas
    slots = shards * replicas
    pos_ref, span_ref, live_ref, bias_ref = refs[:4]
    full = refs[4 : 4 + slots]
    ahead = refs[4 + slots : 4 + 2 * slots]
    outs = refs[4 + 2 * slots : 4 + 2 * slots + shards + replicas]
    rows_out, sums_out = outs[:shards], outs[shards:]
    ks, vs, kt, vt, dk, dv, prob = refs[4 + 2 * slots + shards + replicas :]
    tok = ks.shape[1] // 2
    local = pl.program_id(0)
    head = pos_ref[0] * pl.num_programs(0) + local
    shard, replica, tile = pos_ref[0], pos_ref[1], pos_ref[2]

    def group_of(turn, hop):
        return (shard ^ hop) * replicas + lax.rem(replica + turn, replicas)

    for turn in range(replicas):
        for hop in range(shards):
            slot = turn * shards + hop
            span = span_ref[group_of(turn, hop)]
            for plane, (k, v) in enumerate(
                ((full[slot][2], full[slot][3]), (ahead[slot][0], ahead[slot][1]))
            ):
                part = pl.ds(plane * tok, tok)
                ks[span, part, :] = k
                vs[span, part, :] = v
                kt[span, :, part] = k.T
                vt[span, :, part] = v.T
    dk[...] = jnp.zeros_like(dk)
    dv[...] = jnp.zeros_like(dv)

    def fold(op, x):
        return op(x.reshape(x.shape[0] // 8, 8, x.shape[1]), axis=0)

    def query_tile(hop, count, rows):
        q, g = full[hop][0], full[hop][1]
        scale = inv_root * LOG2E

        def score_step(i, peak):
            s = lax.dot_general(ks[i, :rows, :], q, NT, preferred_element_type=F32)
            s = s * scale + bias_ref[i, head] * LOG2E
            prob[i, :rows, :] = s
            return jnp.maximum(peak, fold(jnp.max, s))

        peak = lax.fori_loop(0, count, score_step, jnp.full((8, tok), -3e38, F32))
        peak = jnp.max(peak, axis=0, keepdims=True)

        def value_step(i, carry):
            total, out = carry
            e = jnp.exp2(prob[i, :rows, :] - peak)
            prob[i, :rows, :] = e
            total = total + fold(jnp.sum, e)
            out = out + jnp.dot(vt[i, :, :rows], e.astype(BF16), preferred_element_type=F32)
            return total, out

        total, out = lax.fori_loop(
            0, count, value_step, (jnp.zeros((8, tok), F32), jnp.zeros((q.shape[1], tok), F32))
        )
        inverse = 1.0 / jnp.sum(total, axis=0, keepdims=True)
        out = (out * inverse).astype(BF16)
        delta = jnp.sum(out.astype(F32) * g.T.astype(F32), axis=0, keepdims=True)
        rows_out[hop][0] = out.T

        def grad_step(i, dq):
            w = prob[i, :rows, :] * inverse
            dp = lax.dot_general(vs[i, :rows, :], g, NT, preferred_element_type=F32)
            ds = (w * (dp - delta) * inv_root).astype(BF16)
            dv[i, :rows, :] += jnp.dot(w.astype(BF16), g, preferred_element_type=F32)
            dk[i, :rows, :] += jnp.dot(ds, q, preferred_element_type=F32)
            return dq + jnp.dot(kt[i, :, :rows], ds, preferred_element_type=F32)

        dq = lax.fori_loop(0, count, grad_step, jnp.zeros((q.shape[1], tok), F32))
        rows_out[hop][1] = dq.astype(BF16).T

    for hop in range(shards):
        group = group_of(0, hop)
        count = span_ref[group] + 1
        live = live_ref[group * tiles + tile]

        @pl.when(live == 1)
        def _():
            query_tile(hop, count, 2 * tok)

        @pl.when(live != 1)
        def _():
            query_tile(hop, count, tok)

    for turn in range(replicas):
        for hop in range(shards):
            span = span_ref[group_of(turn, hop)]
            for plane in range(2):
                part = pl.ds(plane * tok, tok)
                sums_out[turn][hop, 2 * plane] = dk[span, part, :].astype(BF16)
                sums_out[turn][hop, 2 * plane + 1] = dv[span, part, :].astype(BF16)


def merge_kernel(shards, replicas, *refs):
    parts, outs = refs[:replicas], refs[replicas:]
    for hop in range(shards):
        for which in range(4):
            total = parts[0][hop, which].astype(F32)
            for part in parts[1:]:
                total = total + part[hop, which].astype(F32)
            outs[hop if which < 2 else shards + hop][which % 2] = total.astype(BF16)


def unpack_kernel(shards, width, pos_ref, *refs):
    rows, sums, ahead = refs[:shards], refs[shards : 2 * shards], refs[2 * shards : 3 * shards]
    out_ref, dq_ref, dk_ref, dv_ref = refs[3 * shards :]
    shard = pos_ref[0]
    for hop in range(shards):
        lanes = pl.ds(pl.multiple_of((shard ^ hop) * width, 128), width)
        out_ref[:, lanes] = rows[hop][0]
        dq_ref[:, lanes] = rows[hop][1]
        dk_ref[:, lanes] = (sums[hop][0].astype(F32) + ahead[hop][0].astype(F32)).astype(BF16)
        dv_ref[:, lanes] = (sums[hop][1].astype(F32) + ahead[hop][1].astype(F32)).astype(BF16)


def per_device(queries, keys, values, grad_out, span_of_group, noise_level, next_live, level_bias):
    tok, model = queries.shape
    heads = level_bias.shape[1]
    width = model // heads
    groups = lax.axis_size("tm")
    tiles = lax.axis_size("tile")
    shards = shard_count(heads, groups)
    replicas = groups // shards
    own_heads = heads // shards
    cols = own_heads * width
    inv_root = 1.0 / math.sqrt(width)
    me = lax.axis_index("tm")
    shard, replica = me // replicas, me % replicas
    pos = jnp.stack([shard, replica, lax.axis_index("tile")]).astype(jnp.int32)
    shape = jax.ShapeDtypeStruct

    def to_shard(x, hop, lift):
        if hop == 0 and lift == 0:
            return x
        pairs = []
        for t in range(groups):
            goal = ((t // replicas) ^ hop) * replicas + t % replicas
            for s in range(tiles):
                pairs.append((t * tiles + s, goal * tiles + (s + lift) % tiles))
        return lax.ppermute(x, ("tm", "tile"), pairs)

    def to_replica(x, turn):
        pairs = [(t, t // replicas * replicas + (t - turn) % replicas) for t in range(groups)]
        return lax.ppermute(x, "tm", pairs)

    packed = pl.pallas_call(
        functools.partial(pack_kernel, shards, cols),
        out_shape=[shape((4, tok, cols), BF16)] * shards + [shape((2, tok, cols), BF16)] * shards,
        in_specs=[whole(SMEM)] + [whole(VMEM)] * 4,
        out_specs=[whole(VMEM)] * (2 * shards),
        compiler_params=params(32),
        name="pack",
    )(pos, queries, grad_out, keys, values)
    full = [to_shard(packed[hop], hop, 0) for hop in range(shards)]
    ahead = [to_shard(packed[shards + hop], hop, -1) for hop in range(shards)]
    full_all, ahead_all = list(full), list(ahead)
    for turn in range(1, replicas):
        full_all += [to_replica(x, turn) for x in full]
        ahead_all += [to_replica(x, turn) for x in ahead]
    bias = level_bias.at[noise_level].get(mode="promise_in_bounds")

    def head_block(count):
        return pl.BlockSpec((count, tok, width), lambda h: (0, 0, h))

    stacked = pl.BlockSpec((shards, 4, tok, width), lambda h: (0, 0, 0, h))
    results = pl.pallas_call(
        functools.partial(attention_kernel, shards, replicas, tiles, inv_root),
        grid=(own_heads,),
        out_shape=[shape((2, tok, cols), BF16)] * shards
        + [shape((shards, 4, tok, cols), BF16)] * replicas,
        in_specs=[whole(SMEM)] * 4 + [head_block(4)] * groups + [head_block(2)] * groups,
        out_specs=[head_block(2)] * shards + [stacked] * replicas,
        scratch_shapes=[
            VMEM((groups, 2 * tok, width), BF16),
            VMEM((groups, 2 * tok, width), BF16),
            VMEM((groups, width, 2 * tok), BF16),
            VMEM((groups, width, 2 * tok), BF16),
            VMEM((groups, 2 * tok, width), F32),
            VMEM((groups, 2 * tok, width), F32),
            VMEM((groups, 2 * tok, tok), F32),
        ],
        compiler_params=params(48),
        name="attention",
    )(pos, span_of_group, next_live, bias, *full_all, *ahead_all)
    rows, sums = results[:shards], results[shards:]
    rows_home = [to_shard(rows[hop], hop, 0) for hop in range(shards)]
    parts = [sums[0]]
    for turn in range(1, replicas):
        parts.append(to_replica(sums[turn], replicas - turn))
    merged = pl.pallas_call(
        functools.partial(merge_kernel, shards, replicas),
        out_shape=[shape((2, tok, cols), BF16)] * (2 * shards),
        in_specs=[whole(VMEM)] * replicas,
        out_specs=[whole(VMEM)] * (2 * shards),
        compiler_params=params(48),
        name="merge",
    )(*parts)
    sums_home = [to_shard(merged[hop], hop, 0) for hop in range(shards)]
    ahead_home = [to_shard(merged[shards + hop], hop, 1) for hop in range(shards)]
    return pl.pallas_call(
        functools.partial(unpack_kernel, shards, cols),
        out_shape=[shape((tok, model), BF16)] * 4,
        in_specs=[whole(SMEM)] + [whole(VMEM)] * (3 * shards),
        out_specs=[whole(VMEM)] * 4,
        compiler_params=params(32),
        name="unpack",
    )(pos, *rows_home, *sums_home, *ahead_home)


def solution(mesh):
    sharded = P(("tm", "tile"), None)
    return jax.shard_map(
        per_device,
        mesh=mesh,
        in_specs=(sharded,) * 4 + (P(),) * 4,
        out_specs=(sharded,) * 4,
        check_vma=False,
    )
```

time: 364 us -> 132 us (0.36)
  waiting for transfers between devices: 155 us -> 34.2 us
  matrix products: 58.7 us -> 0 us
  Pallas kernels: 0 us -> 49 us
  blocking collectives: 36.2 us -> 0 us
  other arithmetic: 36 us -> 0.67 us
  local copies, waits for them, and re-layouts: 48.7 us -> 15.4 us
  starting transfers between devices: 12.8 us -> 32.4 us
  between operations: 15.1 us -> 0.8 us
    all_gather x8 -> x0, waiting for transfers between devices: 125 us -> none  [the longest x1 34.7 us: per_device(): lax.all_gather(near_v[None], 'tm', axis=0, tiled=True)]
    dot_general x9 -> x0, matrix products: 58.7 us -> none  [the longest x1 10.8 us: per_device(): jnp.einsum('qhe,jkhe->jhqk', grad_heads, all_values, preferred_element_ty...]
    pallas_call x0 -> x4, Pallas kernels: none -> 49 us  [the longest x1 46.1 us: per_device(): pl.pallas_call(functools.partial(attention_kernel, shards, replicas, tile...]
    all_gather x4 -> x0, blocking collectives: 36.2 us -> none  [the longest x1 9.67 us: per_device(): lax.all_gather(near_delta[None], 'tm', axis=0, tiled=True)]
    concatenate x6 -> x0, local copies, waits for them, and re-layouts: 34.5 us -> none  [the longest x1 8.68 us: per_device(): jnp.concatenate([past_q, prev_q], axis=1)]
    concatenate x6 -> x0, other arithmetic: 23.5 us -> none  [the longest x1 5.89 us: per_device(): jnp.concatenate([past_v, ahead_v], axis=1)]
    ppermute x6 -> x26, starting transfers between devices: 12.5 us -> 32.4 us  [the longest x17 31.3 us: to_shard(): return lax.ppermute(x, ('tm', 'tile'), pairs)]
    reduce_sum x5 -> x0, other arithmetic: 11 us -> none  [the longest x1 7.45 us: per_device(): jnp.sum(jnp.exp(scores - row_peak[None, :, :, None]), axis=(0, 3))]
  transfers between devices with their start and end apart: 14 -> 26, of which waited for: 9 -> 13; matrix products, arithmetic and copies ran while one was open for 31% -> 3% of each run, Pallas kernels for 0% -> 0%
where the time goes in v1:
time: 132 us
  Pallas kernels  49 us (37%)
  waiting for transfers between devices  34.2 us (26%)
  starting transfers between devices  32.4 us (25%)
  local copies, waits for them, and re-layouts  15.4 us (12%)
    pallas_call x1, Pallas kernels, per_device(): pl.pallas_call(functools.partial(attention_kernel, shards, replicas, tile...  46.1 us
    ppermute x17, waiting for transfers between devices, to_shard(): return lax.ppermute(x, ('tm', 'tile'), pairs)  34.1 us
    ppermute x17, starting transfers between devices, to_shard(): return lax.ppermute(x, ('tm', 'tile'), pairs)  31.3 us
    unnamed x33, local copies, waits for them, and re-layouts  13.7 us
  transfers between devices with their start and end apart: 26, of which 13 were waited for; matrix products, arithmetic and copies ran while one was open for 3% of the time, Pallas kernels for 0%

profile of v1, /device:TPU:0, one launch (start us, length us, event | category | flops | bytes accessed | tf_op | source)
XLA Modules:
  0.0 132.5 jit_solution(14235527430405089077)
XLA Ops:
  5.5 5.1 %collective-permute-start.7 = (bf16[2,128,384]{2,1,0:T(8,128)(2,1)S(1)}, bf16[2,128,384]{2,1,0:T(8,128)(2,1)S(1)}, u32[]{:S(2)}, u32[]{:S(2)}) collective-permute-start(bf16[2,128,384]{2,1,0:T(8,128)(2,1)S(1)} %get-tuple-element.30), channel_id=1, source_target_pairs={{0,3},{1,0},{2,1},{3,2},{4,7},{5,4},{6,5},{7,6},{8,11},{9,8},{10,9... | collective-permute-start | bytes 589832 | tf_op jit(solution)/shard_map/ppermute | solution.py:192
  12.0 1.4 %collective-permute-start.9 = (bf16[2,128,384]{2,1,0:T(8,128)(2,1)S(1)}, bf16[2,128,384]{2,1,0:T(8,128)(2,1)S(1)}, u32[]{:S(2)}, u32[]{:S(2)}) collective-permute-start(bf16[2,128,384]{2,1,0:T(8,128)(2,1)S(1)} %get-tuple-element.32), channel_id=1, source_target_pairs={{0,19},{1,16},{2,17},{3,18},{4,23},{5,20},{6,21},{7,22},{8,27},{9,... | collective-permute-start | bytes 589832 | tf_op jit(solution)/shard_map/ppermute | solution.py:192
  13.4 1.9 %collective-permute-start = (bf16[4,128,384]{2,1,0:T(8,128)(2,1)S(1)}, bf16[4,128,384]{2,1,0:T(8,128)(2,1)S(1)}, u32[]{:S(2)}, u32[]{:S(2)}) collective-permute-start(bf16[4,128,384]{2,1,0:T(8,128)(2,1)S(1)} %get-tuple-element.27), channel_id=1, source_target_pairs={{0,8},{1,9},{2,10},{3,11},{4,12},{5,13},{6,14},{7,15},{8,0},{9,1},... | collective-permute-start | bytes 1179656 | tf_op jit(solution)/shard_map/ppermute | solution.py:192
  15.9 1.5 %collective-permute-start.1 = (bf16[4,128,384]{2,1,0:T(8,128)(2,1)S(1)}, bf16[4,128,384]{2,1,0:T(8,128)(2,1)S(1)}, u32[]{:S(2)}, u32[]{:S(2)}) collective-permute-start(bf16[4,128,384]{2,1,0:T(8,128)(2,1)S(1)} %get-tuple-element.28), channel_id=1, source_target_pairs={{0,16},{1,17},{2,18},{3,19},{4,20},{5,21},{6,22},{7,23},{8,24},{9,... | collective-permute-start | bytes 1179656 | tf_op jit(solution)/shard_map/ppermute | solution.py:192
  17.4 2.7 %collective-permute-done.8.refs_13_ = bf16[2,128,384]{2,1,0:T(8,128)(2,1)S(1)} collective-permute-done((bf16[2,128,384]{2,1,0:T(8,128)(2,1)S(1)}, bf16[2,128,384]{2,1,0:T(8,128)(2,1)S(1)}, u32[]{:S(2)}, u32[]{:S(2)}) %collective-permute-start.8) | collective-permute-done | bytes 196640 | tf_op jit(solution)/shard_map/ppermute | solution.py:192
  20.1 2.4 %collective-permute-start.2 = (bf16[4,128,384]{2,1,0:T(8,128)(2,1)S(1)}, bf16[4,128,384]{2,1,0:T(8,128)(2,1)S(1)}, u32[]{:S(2)}, u32[]{:S(2)}) collective-permute-start(bf16[4,128,384]{2,1,0:T(8,128)(2,1)S(1)} %get-tuple-element.29), channel_id=1, source_target_pairs={{0,24},{1,25},{2,26},{3,27},{4,28},{5,29},{6,30},{7,31},{8,16},{9,... | collective-permute-start | bytes 1179656 | tf_op jit(solution)/shard_map/ppermute | solution.py:192
  22.6 2.1 %collective-permute-done.9.refs_14_ = bf16[2,128,384]{2,1,0:T(8,128)(2,1)S(1)} collective-permute-done((bf16[2,128,384]{2,1,0:T(8,128)(2,1)S(1)}, bf16[2,128,384]{2,1,0:T(8,128)(2,1)S(1)}, u32[]{:S(2)}, u32[]{:S(2)}) %collective-permute-start.9) | collective-permute-done | bytes 196640 | tf_op jit(solution)/shard_map/ppermute | solution.py:192
  24.6 3.9 %collective-permute-done.10.refs_15_ = bf16[2,128,384]{2,1,0:T(8,128)(2,1)} collective-permute-done((bf16[2,128,384]{2,1,0:T(8,128)(2,1)S(1)}, bf16[2,128,384]{2,1,0:T(8,128)(2,1)}, u32[]{:S(2)}, u32[]{:S(2)}) %collective-permute-start.10) | collective-permute-done | bytes 196640 | tf_op jit(solution)/shard_map/ppermute | solution.py:192
  31.6 10.0 %collective-permute-done.1.refs_6_ = bf16[4,128,384]{2,1,0:T(8,128)(2,1)S(1)} collective-permute-done((bf16[4,128,384]{2,1,0:T(8,128)(2,1)S(1)}, bf16[4,128,384]{2,1,0:T(8,128)(2,1)S(1)}, u32[]{:S(2)}, u32[]{:S(2)}) %collective-permute-start.1) | collective-permute-done | bytes 393248 | tf_op jit(solution)/shard_map/ppermute | solution.py:192
  42.8 1.8 %copy.12 = f32[1000,12]{1,0:T(8,128)} copy(f32[1000,12]{0,1:T(8,128)} %param.15) | data formatting | bytes 96000 | tf_op args[7]
  45.2 1.7 %gather_fusion = f32[8,12]{1,0:T(8,128)S(1)} fusion(f32[1000,12]{1,0:T(8,128)} %copy.12, s32[1024]{0:T(1024)} %pad_clamp_fusion), kind=kCustom, calls=%fused_computation | custom fusion | bytes 800 | tf_op jit(solution)/shard_map/gather | solution.py:212
  50.7 46.1 %attention.1 = (bf16[2,128,384]{2,1,0:T(8,128)(2,1)S(1)}, bf16[2,128,384]{2,1,0:T(8,128)(2,1)S(1)}, bf16[2,128,384]{2,1,0:T(8,128)(2,1)S(1)}, bf16[2,128,384]{2,...) custom-call(s32[3]{0:T(128)S(1)} %pad_add_fusion.pos_ref.refs_0_, ...), custom_call_target="tpu_custom_call" | custom-call | tf_op jit(solution)/shard_map/attention/pallas_call | solution.py:218
  96.9 1.6 %collective-permute-start.15 = (bf16[2,128,384]{2,1,0:T(8,128)(2,1)S(1)}, bf16[2,128,384]{2,1,0:T(8,128)(2,1)S(1)}, u32[]{:S(2)}, u32[]{:S(2)}) collective-permute-start(bf16[2,128,384]{2,1,0:T(8,128)(2,1)S(1)} %get-tuple-element.35), channel_id=1, source_target_pairs={{0,8},{1,9},{2,10},{3,11},{4,12},{5,13},{6,14},{7,15},{8,0},{9,1},... | collective-permute-start | bytes 589832 | tf_op jit(solution)/shard_map/ppermute | solution.py:192
  98.5 1.5 %collective-permute-start.16 = (bf16[2,128,384]{2,1,0:T(8,128)(2,1)S(1)}, bf16[2,128,384]{2,1,0:T(8,128)(2,1)S(1)}, u32[]{:S(2)}, u32[]{:S(2)}) collective-permute-start(bf16[2,128,384]{2,1,0:T(8,128)(2,1)S(1)} %get-tuple-element.36), channel_id=1, source_target_pairs={{0,16},{1,17},{2,18},{3,19},{4,20},{5,21},{6,22},{7,23},{8,24},{9,... | collective-permute-start | bytes 589832 | tf_op jit(solution)/shard_map/ppermute | solution.py:192
  100.5 1.4 %copy-done = bf16[4,4,128,384]{3,2,1,0:T(8,128)(2,1)S(1)} copy-done((bf16[4,4,128,384]{3,2,1,0:T(8,128)(2,1)S(1)}, bf16[4,4,128,384]{3,2,1,0:T(8,128)(2,1)}, u32[]{:S(2)}) %copy-start) | copy-done | bytes 1572888
  102.3 1.6 %collective-permute-start.19 = (bf16[2,128,384]{2,1,0:T(8,128)(2,1)S(1)}, bf16[2,128,384]{2,1,0:T(8,128)(2,1)S(1)}, u32[]{:S(2)}, u32[]{:S(2)}) collective-permute-start(bf16[2,128,384]{2,1,0:T(8,128)(2,1)S(1)} %get-tuple-element.41), channel_id=1, source_target_pairs={{0,8},{1,9},{2,10},{3,11},{4,12},{5,13},{6,14},{7,15},{8,0},{9,1},... | collective-permute-start | bytes 589832 | tf_op jit(solution)/shard_map/ppermute | solution.py:192
  103.9 1.5 %collective-permute-start.20 = (bf16[2,128,384]{2,1,0:T(8,128)(2,1)S(1)}, bf16[2,128,384]{2,1,0:T(8,128)(2,1)S(1)}, u32[]{:S(2)}, u32[]{:S(2)}) collective-permute-start(bf16[2,128,384]{2,1,0:T(8,128)(2,1)S(1)} %get-tuple-element.42), channel_id=1, source_target_pairs={{0,16},{1,17},{2,18},{3,19},{4,20},{5,21},{6,22},{7,23},{8,24},{9,... | collective-permute-start | bytes 589832 | tf_op jit(solution)/shard_map/ppermute | solution.py:192
  105.4 1.7 %collective-permute-start.21 = (bf16[2,128,384]{2,1,0:T(8,128)(2,1)S(1)}, bf16[2,128,384]{2,1,0:T(8,128)(2,1)S(1)}, u32[]{:S(2)}, u32[]{:S(2)}) collective-permute-start(bf16[2,128,384]{2,1,0:T(8,128)(2,1)S(1)} %get-tuple-element.43), channel_id=1, source_target_pairs={{0,24},{1,25},{2,26},{3,27},{4,28},{5,29},{6,30},{7,31},{8,16},{9,... | collective-permute-start | bytes 589832 | tf_op jit(solution)/shard_map/ppermute | solution.py:192
  107.1 2.5 %collective-permute-done.16.refs_2_ = bf16[2,128,384]{2,1,0:T(8,128)(2,1)S(1)} collective-permute-done((bf16[2,128,384]{2,1,0:T(8,128)(2,1)S(1)}, bf16[2,128,384]{2,1,0:T(8,128)(2,1)S(1)}, u32[]{:S(2)}, u32[]{:S(2)}) %collective-permute-start.16) | collective-permute-done | bytes 196640 | tf_op jit(solution)/shard_map/ppermute | solution.py:192
  110.5 2.5 %collective-permute-start.23 = (bf16[2,128,384]{2,1,0:T(8,128)(2,1)S(1)}, bf16[2,128,384]{2,1,0:T(8,128)(2,1)S(1)}, u32[]{:S(2)}, u32[]{:S(2)}) collective-permute-start(bf16[2,128,384]{2,1,0:T(8,128)(2,1)S(1)} %get-tuple-element.45), channel_id=1, source_target_pairs={{0,9},{1,10},{2,11},{3,8},{4,13},{5,14},{6,15},{7,12},{8,1},{9,2},... | collective-permute-start | bytes 589832 | tf_op jit(solution)/shard_map/ppermute | solution.py:192
  113.1 4.1 %collective-permute-start.24 = (bf16[2,128,384]{2,1,0:T(8,128)(2,1)S(1)}, bf16[2,128,384]{2,1,0:T(8,128)(2,1)S(1)}, u32[]{:S(2)}, u32[]{:S(2)}) collective-permute-start(bf16[2,128,384]{2,1,0:T(8,128)(2,1)S(1)} %get-tuple-element.46), channel_id=1, source_target_pairs={{0,17},{1,18},{2,19},{3,16},{4,21},{5,22},{6,23},{7,20},{8,25},{9,... | collective-permute-start | bytes 589832 | tf_op jit(solution)/shard_map/ppermute | solution.py:192
  117.2 1.7 %collective-permute-start.25 = (bf16[2,128,384]{2,1,0:T(8,128)(2,1)S(1)}, bf16[2,128,384]{2,1,0:T(8,128)(2,1)S(1)}, u32[]{:S(2)}, u32[]{:S(2)}) collective-permute-start(bf16[2,128,384]{2,1,0:T(8,128)(2,1)S(1)} %get-tuple-element.47), channel_id=1, source_target_pairs={{0,25},{1,26},{2,27},{3,24},{4,29},{5,30},{6,31},{7,28},{8,17},{9,... | collective-permute-start | bytes 589832 | tf_op jit(solution)/shard_map/ppermute | solution.py:192
  121.0 8.6 %collective-permute-done.24.refs_10_ = bf16[2,128,384]{2,1,0:T(8,128)(2,1)S(1)} collective-permute-done((bf16[2,128,384]{2,1,0:T(8,128)(2,1)S(1)}, bf16[2,128,384]{2,1,0:T(8,128)(2,1)S(1)}, u32[]{:S(2)}, u32[]{:S(2)}) %collective-permute-start.24) | collective-permute-done | bytes 196640 | tf_op jit(solution)/shard_map/ppermute | solution.py:192
  130.7 1.8 %unpack.1 = (bf16[128,1536]{1,0:T(8,128)(2,1)}, bf16[128,1536]{1,0:T(8,128)(2,1)}, bf16[128,1536]{1,0:T(8,128)(2,1)}, bf16[128,1536]{1,0:T(8,128)(2,1)}) custom-call(s32[3]{0:T(128)S(1)} %pad_add_fusion.pos_ref.refs_0_, bf16[2,128,384]{2,1,0:T(8,128)(2,1)S(1)} %get-tuple-element.34.refs_0_, bf16[2,128,384]{2,1,0:T(8,128)(2,1)S(1)} %collective-permute-done.15.refs_1_, ...), custom_call_target="tpu_custom_call" | custom-call | tf_op jit(solution)/shard_map/unpack/pallas_call | solution.py:252
  (69 shorter events, 20.4 us)
Async XLA Ops:
  5.5 10.4 %collective-permute-start.7 = (bf16[2,128,384]{2,1,0:T(8,128)(2,1)S(1)}, bf16[2,128,384]{2,1,0:T(8,128)(2,1)S(1)}, u32[]{:S(2)}, u32[]{:S(2)}) collective-permute-start(bf16[2,128,384]{2,1,0:T(8,128)(2,1)S(1)} %get-tuple-element.30), channel_id=1, source_target_pairs={{0,3},{1,0},{2,1},{3,2},{4,7},{5,4},{6,5},{7,6},{8,11},{9,8},{10,9... | collective-permute-start | bytes 589832 | tf_op jit(solution)/shard_map/ppermute | solution.py:192
  10.6 9.5 %collective-permute-start.8 = (bf16[2,128,384]{2,1,0:T(8,128)(2,1)S(1)}, bf16[2,128,384]{2,1,0:T(8,128)(2,1)S(1)}, u32[]{:S(2)}, u32[]{:S(2)}) collective-permute-start(bf16[2,128,384]{2,1,0:T(8,128)(2,1)S(1)} %get-tuple-element.31), channel_id=1, source_target_pairs={{0,11},{1,8},{2,9},{3,10},{4,15},{5,12},{6,13},{7,14},{8,3},{9,0},... | collective-permute-start | bytes 589832 | tf_op jit(solution)/shard_map/ppermute | solution.py:192
  12.0 12.6 %collective-permute-start.9 = (bf16[2,128,384]{2,1,0:T(8,128)(2,1)S(1)}, bf16[2,128,384]{2,1,0:T(8,128)(2,1)S(1)}, u32[]{:S(2)}, u32[]{:S(2)}) collective-permute-start(bf16[2,128,384]{2,1,0:T(8,128)(2,1)S(1)} %get-tuple-element.32), channel_id=1, source_target_pairs={{0,19},{1,16},{2,17},{3,18},{4,23},{5,20},{6,21},{7,22},{8,27},{9,... | collective-permute-start | bytes 589832 | tf_op jit(solution)/shard_map/ppermute | solution.py:192
  13.4 15.1 %collective-permute-start.10 = (bf16[2,128,384]{2,1,0:T(8,128)(2,1)S(1)}, bf16[2,128,384]{2,1,0:T(8,128)(2,1)}, u32[]{:S(2)}, u32[]{:S(2)}) collective-permute-start(bf16[2,128,384]{2,1,0:T(8,128)(2,1)S(1)} %get-tuple-element.33), channel_id=1, source_target_pairs={{0,27},{1,24},{2,25},{3,26},{4,31},{5,28},{6,29},{7,30},{8,19},{9,... | collective-permute-start | bytes 589832 | tf_op jit(solution)/shard_map/ppermute | solution.py:192
  13.4 18.1 %collective-permute-start = (bf16[4,128,384]{2,1,0:T(8,128)(2,1)S(1)}, bf16[4,128,384]{2,1,0:T(8,128)(2,1)S(1)}, u32[]{:S(2)}, u32[]{:S(2)}) collective-permute-start(bf16[4,128,384]{2,1,0:T(8,128)(2,1)S(1)} %get-tuple-element.27), channel_id=1, source_target_pairs={{0,8},{1,9},{2,10},{3,11},{4,12},{5,13},{6,14},{7,15},{8,0},{9,1},... | collective-permute-start | bytes 1179656 | tf_op jit(solution)/shard_map/ppermute | solution.py:192
  15.9 25.7 %collective-permute-start.1 = (bf16[4,128,384]{2,1,0:T(8,128)(2,1)S(1)}, bf16[4,128,384]{2,1,0:T(8,128)(2,1)S(1)}, u32[]{:S(2)}, u32[]{:S(2)}) collective-permute-start(bf16[4,128,384]{2,1,0:T(8,128)(2,1)S(1)} %get-tuple-element.28), channel_id=1, source_target_pairs={{0,16},{1,17},{2,18},{3,19},{4,20},{5,21},{6,22},{7,23},{8,24},{9,... | collective-permute-start | bytes 1179656 | tf_op jit(solution)/shard_map/ppermute | solution.py:192
  20.1 21.5 %collective-permute-start.2 = (bf16[4,128,384]{2,1,0:T(8,128)(2,1)S(1)}, bf16[4,128,384]{2,1,0:T(8,128)(2,1)S(1)}, u32[]{:S(2)}, u32[]{:S(2)}) collective-permute-start(bf16[4,128,384]{2,1,0:T(8,128)(2,1)S(1)} %get-tuple-element.29), channel_id=1, source_target_pairs={{0,24},{1,25},{2,26},{3,27},{4,28},{5,29},{6,30},{7,31},{8,16},{9,... | collective-permute-start | bytes 1179656 | tf_op jit(solution)/shard_map/ppermute | solution.py:192
  24.6 3.9 %collective-permute-start.11 = (bf16[2,128,384]{2,1,0:T(8,128)(2,1)S(1)}, bf16[2,128,384]{2,1,0:T(8,128)(2,1)S(1)}, u32[]{:S(2)}, u32[]{:S(2)}) collective-permute-start(bf16[2,128,384]{2,1,0:T(8,128)(2,1)S(1)} %collective-permute-done.7.refs_12_), channel_id=1, source_target_pairs={{0,4},{4,0},{8,12},{12,8},{16,20},{20,16},{24,28},{28,24},{1,5},{5... | collective-permute-start | bytes 589832 | tf_op jit(solution)/shard_map/ppermute | solution.py:196
  29.2 12.9 %collective-permute-start.13 = (bf16[2,128,384]{2,1,0:T(8,128)(2,1)S(1)}, bf16[2,128,384]{2,1,0:T(8,128)(2,1)S(1)}, u32[]{:S(2)}, u32[]{:S(2)}) collective-permute-start(bf16[2,128,384]{2,1,0:T(8,128)(2,1)S(1)} %collective-permute-done.9.refs_14_), channel_id=1, source_target_pairs={{0,4},{4,0},{8,12},{12,8},{16,20},{20,16},{24,28},{28,24},{1,5},{5... | collective-permute-start | bytes 589832 | tf_op jit(solution)/shard_map/ppermute | solution.py:196
  31.1 15.9 %collective-permute-start.3 = (bf16[4,128,384]{2,1,0:T(8,128)(2,1)S(1)}, bf16[4,128,384]{2,1,0:T(8,128)(2,1)S(1)}, u32[]{:S(2)}, u32[]{:S(2)}) collective-permute-start(bf16[4,128,384]{2,1,0:T(8,128)(2,1)S(1)} %get-tuple-element.26.refs_4_), channel_id=1, source_target_pairs={{0,4},{4,0},{8,12},{12,8},{16,20},{20,16},{24,28},{28,24},{1,5},{5... | collective-permute-start | bytes 1179656 | tf_op jit(solution)/shard_map/ppermute | solution.py:196
  31.5 15.5 %collective-permute-start.4 = (bf16[4,128,384]{2,1,0:T(8,128)(2,1)S(1)}, bf16[4,128,384]{2,1,0:T(8,128)(2,1)S(1)}, u32[]{:S(2)}, u32[]{:S(2)}) collective-permute-start(bf16[4,128,384]{2,1,0:T(8,128)(2,1)S(1)} %collective-permute-done.refs_5_), channel_id=1, source_target_pairs={{0,4},{4,0},{8,12},{12,8},{16,20},{20,16},{24,28},{28,24},{1,5},{5... | collective-permute-start | bytes 1179656 | tf_op jit(solution)/shard_map/ppermute | solution.py:196
  41.6 5.4 %collective-permute-start.5 = (bf16[4,128,384]{2,1,0:T(8,128)(2,1)S(1)}, bf16[4,128,384]{2,1,0:T(8,128)(2,1)S(1)}, u32[]{:S(2)}, u32[]{:S(2)}) collective-permute-start(bf16[4,128,384]{2,1,0:T(8,128)(2,1)S(1)} %collective-permute-done.1.refs_6_), channel_id=1, source_target_pairs={{0,4},{4,0},{8,12},{12,8},{16,20},{20,16},{24,28},{28,24},{1,5},{5... | collective-permute-start | bytes 1179656 | tf_op jit(solution)/shard_map/ppermute | solution.py:196
  41.6 5.4 %collective-permute-start.6 = (bf16[4,128,384]{2,1,0:T(8,128)(2,1)S(1)}, bf16[4,128,384]{2,1,0:T(8,128)(2,1)S(1)}, u32[]{:S(2)}, u32[]{:S(2)}) collective-permute-start(bf16[4,128,384]{2,1,0:T(8,128)(2,1)S(1)} %collective-permute-done.2.refs_7_), channel_id=1, source_target_pairs={{0,4},{4,0},{8,12},{12,8},{16,20},{20,16},{24,28},{28,24},{1,5},{5... | collective-permute-start | bytes 1179656 | tf_op jit(solution)/shard_map/ppermute | solution.py:196
  42.8 4.2 %collective-permute-start.14 = (bf16[2,128,384]{2,1,0:T(8,128)(2,1)}, bf16[2,128,384]{2,1,0:T(8,128)(2,1)}, u32[]{:S(2)}, u32[]{:S(2)}) collective-permute-start(bf16[2,128,384]{2,1,0:T(8,128)(2,1)} %collective-permute-done.10.refs_15_), channel_id=1, source_target_pairs={{0,4},{4,0},{8,12},{12,8},{16,20},{20,16},{24,28},{28,24},{1,5},{5... | collective-permute-start | bytes 589832 | tf_op jit(solution)/shard_map/ppermute | solution.py:196
  96.9 8.5 %collective-permute-start.15 = (bf16[2,128,384]{2,1,0:T(8,128)(2,1)S(1)}, bf16[2,128,384]{2,1,0:T(8,128)(2,1)S(1)}, u32[]{:S(2)}, u32[]{:S(2)}) collective-permute-start(bf16[2,128,384]{2,1,0:T(8,128)(2,1)S(1)} %get-tuple-element.35), channel_id=1, source_target_pairs={{0,8},{1,9},{2,10},{3,11},{4,12},{5,13},{6,14},{7,15},{8,0},{9,1},... | collective-permute-start | bytes 589832 | tf_op jit(solution)/shard_map/ppermute | solution.py:192
  98.5 11.2 %collective-permute-start.16 = (bf16[2,128,384]{2,1,0:T(8,128)(2,1)S(1)}, bf16[2,128,384]{2,1,0:T(8,128)(2,1)S(1)}, u32[]{:S(2)}, u32[]{:S(2)}) collective-permute-start(bf16[2,128,384]{2,1,0:T(8,128)(2,1)S(1)} %get-tuple-element.36), channel_id=1, source_target_pairs={{0,16},{1,17},{2,18},{3,19},{4,20},{5,21},{6,22},{7,23},{8,24},{9,... | collective-permute-start | bytes 589832 | tf_op jit(solution)/shard_map/ppermute | solution.py:192
  100.0 10.5 %collective-permute-start.17 = (bf16[2,128,384]{2,1,0:T(8,128)(2,1)S(1)}, bf16[2,128,384]{2,1,0:T(8,128)(2,1)S(1)}, u32[]{:S(2)}, u32[]{:S(2)}) collective-permute-start(bf16[2,128,384]{2,1,0:T(8,128)(2,1)S(1)} %get-tuple-element.37), channel_id=1, source_target_pairs={{0,24},{1,25},{2,26},{3,27},{4,28},{5,29},{6,30},{7,31},{8,16},{9,... | collective-permute-start | bytes 589832 | tf_op jit(solution)/shard_map/ppermute | solution.py:192
  102.3 10.8 %collective-permute-start.19 = (bf16[2,128,384]{2,1,0:T(8,128)(2,1)S(1)}, bf16[2,128,384]{2,1,0:T(8,128)(2,1)S(1)}, u32[]{:S(2)}, u32[]{:S(2)}) collective-permute-start(bf16[2,128,384]{2,1,0:T(8,128)(2,1)S(1)} %get-tuple-element.41), channel_id=1, source_target_pairs={{0,8},{1,9},{2,10},{3,11},{4,12},{5,13},{6,14},{7,15},{8,0},{9,1},... | collective-permute-start | bytes 589832 | tf_op jit(solution)/shard_map/ppermute | solution.py:192
  103.9 13.4 %collective-permute-start.20 = (bf16[2,128,384]{2,1,0:T(8,128)(2,1)S(1)}, bf16[2,128,384]{2,1,0:T(8,128)(2,1)S(1)}, u32[]{:S(2)}, u32[]{:S(2)}) collective-permute-start(bf16[2,128,384]{2,1,0:T(8,128)(2,1)S(1)} %get-tuple-element.42), channel_id=1, source_target_pairs={{0,16},{1,17},{2,18},{3,19},{4,20},{5,21},{6,22},{7,23},{8,24},{9,... | collective-permute-start | bytes 589832 | tf_op jit(solution)/shard_map/ppermute | solution.py:192
  105.4 14.6 %collective-permute-start.21 = (bf16[2,128,384]{2,1,0:T(8,128)(2,1)S(1)}, bf16[2,128,384]{2,1,0:T(8,128)(2,1)S(1)}, u32[]{:S(2)}, u32[]{:S(2)}) collective-permute-start(bf16[2,128,384]{2,1,0:T(8,128)(2,1)S(1)} %get-tuple-element.43), channel_id=1, source_target_pairs={{0,24},{1,25},{2,26},{3,27},{4,28},{5,29},{6,30},{7,31},{8,16},{9,... | collective-permute-start | bytes 589832 | tf_op jit(solution)/shard_map/ppermute | solution.py:192
  109.6 10.4 %collective-permute-start.22 = (bf16[2,128,384]{2,1,0:T(8,128)(2,1)S(1)}, bf16[2,128,384]{2,1,0:T(8,128)(2,1)S(1)}, u32[]{:S(2)}, u32[]{:S(2)}) collective-permute-start(bf16[2,128,384]{2,1,0:T(8,128)(2,1)S(1)} %get-tuple-element.44), channel_id=1, source_target_pairs={{0,1},{1,2},{2,3},{3,0},{4,5},{5,6},{6,7},{7,4},{8,9},{9,10},{10,1... | collective-permute-start | bytes 589832 | tf_op jit(solution)/shard_map/ppermute | solution.py:192
  110.5 10.5 %collective-permute-start.23 = (bf16[2,128,384]{2,1,0:T(8,128)(2,1)S(1)}, bf16[2,128,384]{2,1,0:T(8,128)(2,1)S(1)}, u32[]{:S(2)}, u32[]{:S(2)}) collective-permute-start(bf16[2,128,384]{2,1,0:T(8,128)(2,1)S(1)} %get-tuple-element.45), channel_id=1, source_target_pairs={{0,9},{1,10},{2,11},{3,8},{4,13},{5,14},{6,15},{7,12},{8,1},{9,2},... | collective-permute-start | bytes 589832 | tf_op jit(solution)/shard_map/ppermute | solution.py:192
  113.1 16.6 %collective-permute-start.24 = (bf16[2,128,384]{2,1,0:T(8,128)(2,1)S(1)}, bf16[2,128,384]{2,1,0:T(8,128)(2,1)S(1)}, u32[]{:S(2)}, u32[]{:S(2)}) collective-permute-start(bf16[2,128,384]{2,1,0:T(8,128)(2,1)S(1)} %get-tuple-element.46), channel_id=1, source_target_pairs={{0,17},{1,18},{2,19},{3,16},{4,21},{5,22},{6,23},{7,20},{8,25},{9,... | collective-permute-start | bytes 589832 | tf_op jit(solution)/shard_map/ppermute | solution.py:192
  117.2 13.4 %collective-permute-start.25 = (bf16[2,128,384]{2,1,0:T(8,128)(2,1)S(1)}, bf16[2,128,384]{2,1,0:T(8,128)(2,1)S(1)}, u32[]{:S(2)}, u32[]{:S(2)}) collective-permute-start(bf16[2,128,384]{2,1,0:T(8,128)(2,1)S(1)} %get-tuple-element.47), channel_id=1, source_target_pairs={{0,25},{1,26},{2,27},{3,24},{4,29},{5,30},{6,31},{7,28},{8,17},{9,... | collective-permute-start | bytes 589832 | tf_op jit(solution)/shard_map/ppermute | solution.py:192
  (18 other events, 152.2 us)

commit v2 on v1

--- a/solution.py
+++ b/solution.py
@@ -46,80 +46,97 @@
         pair[1] = v
 
 
-def attention_kernel(shards, replicas, tiles, inv_root, *refs):
-    groups = shards * replicas
+def attention_kernel(shards, replicas, tiles, own_heads, batch, inv_root, *refs):
     slots = shards * replicas
     pos_ref, span_ref, live_ref, bias_ref = refs[:4]
     full = refs[4 : 4 + slots]
     ahead = refs[4 + slots : 4 + 2 * slots]
     outs = refs[4 + 2 * slots : 4 + 2 * slots + shards + replicas]
     rows_out, sums_out = outs[:shards], outs[shards:]
-    ks, vs, kt, vt, dk, dv, prob = refs[4 + 2 * slots + shards + replicas :]
-    tok = ks.shape[1] // 2
-    local = pl.program_id(0)
-    head = pos_ref[0] * pl.num_programs(0) + local
+    kv, kt, vt, acc, score, dprob, both, ot, dqt = refs[4 + 2 * slots + shards + replicas :]
+    tok, width = kv.shape[2] // 2, kv.shape[3] // 2
     shard, replica, tile = pos_ref[0], pos_ref[1], pos_ref[2]
+    first = shard * own_heads + pl.program_id(0) * batch
+    heads = range(batch)
+    scale = inv_root * LOG2E
 
     def group_of(turn, hop):
         return (shard ^ hop) * replicas + lax.rem(replica + turn, replicas)
+
+    def lanes(h):
+        return pl.ds(h * width, width)
 
     for turn in range(replicas):
         for hop in range(shards):
             slot = turn * shards + hop
             span = span_ref[group_of(turn, hop)]
-            for plane, (k, v) in enumerate(
-                ((full[slot][2], full[slot][3]), (ahead[slot][0], ahead[slot][1]))
-            ):
-                part = pl.ds(plane * tok, tok)
-                ks[span, part, :] = k
-                vs[span, part, :] = v
-                kt[span, :, part] = k.T
-                vt[span, :, part] = v.T
-    dk[...] = jnp.zeros_like(dk)
-    dv[...] = jnp.zeros_like(dv)
+            for h in heads:
+                for plane, (ref, at) in enumerate(((full[slot], 2), (ahead[slot], 0))):
+                    part = pl.ds(plane * tok, tok)
+                    k, v = ref[at, :, lanes(h)], ref[at + 1, :, lanes(h)]
+                    kv[h, span, part, :width] = k
+                    kv[h, span, part, width:] = v
+                    kt[h, span, :, part] = k.T
+                    vt[h, span, :, part] = v.T
+    acc[...] = jnp.zeros_like(acc)
+    both[...] = jnp.zeros_like(both)
 
     def fold(op, x):
         return op(x.reshape(x.shape[0] // 8, 8, x.shape[1]), axis=0)
 
     def query_tile(hop, count, rows):
-        q, g = full[hop][0], full[hop][1]
-        scale = inv_root * LOG2E
-
-        def score_step(i, peak):
-            s = lax.dot_general(ks[i, :rows, :], q, NT, preferred_element_type=F32)
-            s = s * scale + bias_ref[i, head] * LOG2E
-            prob[i, :rows, :] = s
-            return jnp.maximum(peak, fold(jnp.max, s))
-
-        peak = lax.fori_loop(0, count, score_step, jnp.full((8, tok), -3e38, F32))
-        peak = jnp.max(peak, axis=0, keepdims=True)
-
-        def value_step(i, carry):
-            total, out = carry
-            e = jnp.exp2(prob[i, :rows, :] - peak)
-            prob[i, :rows, :] = e
-            total = total + fold(jnp.sum, e)
-            out = out + jnp.dot(vt[i, :, :rows], e.astype(BF16), preferred_element_type=F32)
-            return total, out
-
-        total, out = lax.fori_loop(
-            0, count, value_step, (jnp.zeros((8, tok), F32), jnp.zeros((q.shape[1], tok), F32))
+        for h in heads:
+            both[h, :tok, :width] = full[hop][0, :, lanes(h)]
+            both[h, tok:, width:] = full[hop][1, :, lanes(h)]
+        ot[...] = jnp.zeros_like(ot)
+        dqt[...] = jnp.zeros_like(dqt)
+
+        def score_step(i, peaks):
+            new = []
+            for h in heads:
+                sd = lax.dot_general(kv[h, i, :rows, :], both[h], NT, preferred_element_type=F32)
+                s = sd[:, :tok] * scale + bias_ref[i, first + h] * LOG2E
+                score[h, i, :rows, :] = s
+                dprob[h, i, :rows, :] = sd[:, tok:]
+                new.append(jnp.maximum(peaks[h], fold(jnp.max, s)))
+            return tuple(new)
+
+        peaks = lax.fori_loop(
+            0, count, score_step, tuple(jnp.full((8, tok), -3e38, F32) for _ in heads)
         )
-        inverse = 1.0 / jnp.sum(total, axis=0, keepdims=True)
-        out = (out * inverse).astype(BF16)
-        delta = jnp.sum(out.astype(F32) * g.T.astype(F32), axis=0, keepdims=True)
-        rows_out[hop][0] = out.T
-
-        def grad_step(i, dq):
-            w = prob[i, :rows, :] * inverse
-            dp = lax.dot_general(vs[i, :rows, :], g, NT, preferred_element_type=F32)
-            ds = (w * (dp - delta) * inv_root).astype(BF16)
-            dv[i, :rows, :] += jnp.dot(w.astype(BF16), g, preferred_element_type=F32)
-            dk[i, :rows, :] += jnp.dot(ds, q, preferred_element_type=F32)
-            return dq + jnp.dot(kt[i, :, :rows], ds, preferred_element_type=F32)
-
-        dq = lax.fori_loop(0, count, grad_step, jnp.zeros((q.shape[1], tok), F32))
-        rows_out[hop][1] = dq.astype(BF16).T
+        peaks = [jnp.max(x, axis=0, keepdims=True) for x in peaks]
+
+        def total_step(i, carry):
+            new = []
+            for h in heads:
+                e = jnp.exp2(score[h, i, :rows, :] - peaks[h])
+                new.append(carry[2 * h] + fold(jnp.sum, e))
+                new.append(carry[2 * h + 1] + fold(jnp.sum, e * dprob[h, i, :rows, :]))
+            return tuple(new)
+
+        totals = lax.fori_loop(
+            0, count, total_step, tuple(jnp.zeros((8, tok), F32) for _ in range(2 * batch))
+        )
+        totals = [jnp.sum(x, axis=0, keepdims=True) for x in totals]
+        log_total = [peaks[h] + jnp.log2(totals[2 * h]) for h in heads]
+        delta = [totals[2 * h + 1] / totals[2 * h] for h in heads]
+
+        def grad_step(i, carry):
+            for h in heads:
+                w = jnp.exp2(score[h, i, :rows, :] - log_total[h])
+                ds = (w * (dprob[h, i, :rows, :] - delta[h])).astype(BF16)
+                w = w.astype(BF16)
+                acc[h, i, :rows, :] += jnp.dot(
+                    jnp.concatenate([ds, w], axis=1), both[h], preferred_element_type=F32
+                )
+                ot[h] += jnp.dot(vt[h, i, :, :rows], w, preferred_element_type=F32)
+                dqt[h] += jnp.dot(kt[h, i, :, :rows], ds, preferred_element_type=F32)
+            return carry
+
+        lax.fori_loop(0, count, grad_step, 0)
+        for h in heads:
+            rows_out[hop][0, :, lanes(h)] = ot[h].astype(BF16).T
+            rows_out[hop][1, :, lanes(h)] = (dqt[h] * inv_root).astype(BF16).T
 
     for hop in range(shards):
         group = group_of(0, hop)
@@ -137,10 +154,15 @@
     for turn in range(replicas):
         for hop in range(shards):
             span = span_ref[group_of(turn, hop)]
-            for plane in range(2):
-                part = pl.ds(plane * tok, tok)
-                sums_out[turn][hop, 2 * plane] = dk[span, part, :].astype(BF16)
-                sums_out[turn][hop, 2 * plane + 1] = dv[span, part, :].astype(BF16)
+            for h in heads:
+                for plane in range(2):
+                    part = pl.ds(plane * tok, tok)
+                    sums_out[turn][hop, 2 * plane, :, lanes(h)] = (
+                        acc[h, span, part, :width] * inv_root
+                    ).astype(BF16)
+                    sums_out[turn][hop, 2 * plane + 1, :, lanes(h)] = acc[
+                        h, span, part, width:
+                    ].astype(BF16)
 
 
 def merge_kernel(shards, replicas, *refs):
@@ -163,6 +185,42 @@
         dq_ref[:, lanes] = rows[hop][1]
         dk_ref[:, lanes] = (sums[hop][0].astype(F32) + ahead[hop][0].astype(F32)).astype(BF16)
         dv_ref[:, lanes] = (sums[hop][1].astype(F32) + ahead[hop][1].astype(F32)).astype(BF16)
+
+
+def attend(sizes, pos, span_of_group, next_live, bias, full, ahead):
+    shards, replicas, tiles, own_heads, width, tok = sizes
+    groups = shards * replicas
+    batch = own_heads if groups <= 8 else 1
+    cols, step = own_heads * width, batch * width
+    shape = jax.ShapeDtypeStruct
+
+    def head_block(count):
+        return pl.BlockSpec((count, tok, step), lambda h: (0, 0, h))
+
+    stacked = pl.BlockSpec((shards, 4, tok, step), lambda h: (0, 0, 0, h))
+    return pl.pallas_call(
+        functools.partial(
+            attention_kernel, shards, replicas, tiles, own_heads, batch, 1.0 / math.sqrt(width)
+        ),
+        grid=(own_heads // batch,),
+        out_shape=[shape((2, tok, cols), BF16)] * shards
+        + [shape((shards, 4, tok, cols), BF16)] * replicas,
+        in_specs=[whole(SMEM)] * 4 + [head_block(4)] * groups + [head_block(2)] * groups,
+        out_specs=[head_block(2)] * shards + [stacked] * replicas,
+        scratch_shapes=[
+            VMEM((batch, groups, 2 * tok, 2 * width), BF16),
+            VMEM((batch, groups, width, 2 * tok), BF16),
+            VMEM((batch, groups, width, 2 * tok), BF16),
+            VMEM((batch, groups, 2 * tok, 2 * width), F32),
+            VMEM((batch, groups, 2 * tok, tok), F32),
+            VMEM((batch, groups, 2 * tok, tok), F32),
+            VMEM((batch, 2 * tok, 2 * width), BF16),
+            VMEM((batch, width, tok), F32),
+            VMEM((batch, width, tok), F32),
+        ],
+        compiler_params=params(48),
+        name="attention",
+    )(pos, span_of_group, next_live, bias, *full, *ahead)
 
 
 def per_device(queries, keys, values, grad_out, span_of_group, noise_level, next_live, level_bias):
@@ -211,29 +269,10 @@
         ahead_all += [to_replica(x, turn) for x in ahead]
     bias = level_bias.at[noise_level].get(mode="promise_in_bounds")
 
-    def head_block(count):
-        return pl.BlockSpec((count, tok, width), lambda h: (0, 0, h))
-
-    stacked = pl.BlockSpec((shards, 4, tok, width), lambda h: (0, 0, 0, h))
-    results = pl.pallas_call(
-        functools.partial(attention_kernel, shards, replicas, tiles, inv_root),
-        grid=(own_heads,),
-        out_shape=[shape((2, tok, cols), BF16)] * shards
-        + [shape((shards, 4, tok, cols), BF16)] * replicas,
-        in_specs=[whole(SMEM)] * 4 + [head_block(4)] * groups + [head_block(2)] * groups,
-        out_specs=[head_block(2)] * shards + [stacked] * replicas,
-        scratch_shapes=[
-            VMEM((groups, 2 * tok, width), BF16),
-            VMEM((groups, 2 * tok, width), BF16),
-            VMEM((groups, width, 2 * tok), BF16),
-            VMEM((groups, width, 2 * tok), BF16),
-            VMEM((groups, 2 * tok, width), F32),
-            VMEM((groups, 2 * tok, width), F32),
-            VMEM((groups, 2 * tok, tok), F32),
-        ],
-        compiler_params=params(48),
-        name="attention",
-    )(pos, span_of_group, next_live, bias, *full_all, *ahead_all)
+    results = attend(
+        (shards, replicas, tiles, own_heads, width, tok),
+        pos, span_of_group, next_live, bias, full_all, ahead_all,
+    )
     rows, sums = results[:shards], results[shards:]
     rows_home = [to_shard(rows[hop], hop, 0) for hop in range(shards)]
     parts = [sums[0]]

time: 132 us -> 110 us (0.83); the launches traced: 132 us -> 108 us
  Pallas kernels: 49 us -> 22.4 us
  waiting for transfers between devices: 34.2 us -> 35.9 us
    pallas_call x1, Pallas kernels: 46.1 us -> 19.5 us  [attend(): pl.pallas_call(functools.partial(attention_kernel, shards, replicas, tile...]
    ppermute x17, waiting for transfers between devices: 34.1 us -> 35.8 us  [to_shard(): return lax.ppermute(x, ('tm', 'tile'), pairs)]
  transfers between devices with their start and end apart: 26 -> 26, of which waited for: 13 -> 12; matrix products, arithmetic and copies ran while one was open for 3% -> 4% of each run, Pallas kernels for 0% -> 0%
where the time goes in v2:
time: 110 us; the launch traced here: 108 us
  waiting for transfers between devices  35.9 us (33%)
  starting transfers between devices  33.3 us (30%)
  Pallas kernels  22.4 us (20%)
  local copies, waits for them, and re-layouts  15.4 us (14%)
    ppermute x17, waiting for transfers between devices, to_shard(): return lax.ppermute(x, ('tm', 'tile'), pairs)  35.8 us
    ppermute x17, starting transfers between devices, to_shard(): return lax.ppermute(x, ('tm', 'tile'), pairs)  32.2 us
    pallas_call x1, Pallas kernels, attend(): pl.pallas_call(functools.partial(attention_kernel, shards, replicas, tile...  19.5 us
    unnamed x33, local copies, waits for them, and re-layouts  13.6 us
  transfers between devices with their start and end apart: 26, of which 12 were waited for; matrix products, arithmetic and copies ran while one was open for 4% of the time, Pallas kernels for 0%

profile of v2, /device:TPU:0, one launch (start us, length us, event | category | flops | bytes accessed | tf_op | source)
XLA Modules:
  0.0 108.4 jit_solution(5669715257698563550)
XLA Ops:
  5.5 5.1 %collective-permute-start.7 = (bf16[2,128,384]{2,1,0:T(8,128)(2,1)S(1)}, bf16[2,128,384]{2,1,0:T(8,128)(2,1)S(1)}, u32[]{:S(2)}, u32[]{:S(2)}) collective-permute-start(bf16[2,128,384]{2,1,0:T(8,128)(2,1)S(1)} %get-tuple-element.30), channel_id=1, source_target_pairs={{0,3},{1,0},{2,1},{3,2},{4,7},{5,4},{6,5},{7,6},{8,11},{9,8},{10,9... | collective-permute-start | bytes 589832 | tf_op jit(solution)/shard_map/ppermute | solution.py:250
  13.4 1.9 %collective-permute-start = (bf16[4,128,384]{2,1,0:T(8,128)(2,1)S(1)}, bf16[4,128,384]{2,1,0:T(8,128)(2,1)S(1)}, u32[]{:S(2)}, u32[]{:S(2)}) collective-permute-start(bf16[4,128,384]{2,1,0:T(8,128)(2,1)S(1)} %get-tuple-element.27), channel_id=1, source_target_pairs={{0,8},{1,9},{2,10},{3,11},{4,12},{5,13},{6,14},{7,15},{8,0},{9,1},... | collective-permute-start | bytes 1179656 | tf_op jit(solution)/shard_map/ppermute | solution.py:250
  15.9 1.5 %collective-permute-start.1 = (bf16[4,128,384]{2,1,0:T(8,128)(2,1)S(1)}, bf16[4,128,384]{2,1,0:T(8,128)(2,1)S(1)}, u32[]{:S(2)}, u32[]{:S(2)}) collective-permute-start(bf16[4,128,384]{2,1,0:T(8,128)(2,1)S(1)} %get-tuple-element.28), channel_id=1, source_target_pairs={{0,16},{1,17},{2,18},{3,19},{4,20},{5,21},{6,22},{7,23},{8,24},{9,... | collective-permute-start | bytes 1179656 | tf_op jit(solution)/shard_map/ppermute | solution.py:250
  17.4 2.7 %collective-permute-done.8.refs_13_ = bf16[2,128,384]{2,1,0:T(8,128)(2,1)S(1)} collective-permute-done((bf16[2,128,384]{2,1,0:T(8,128)(2,1)S(1)}, bf16[2,128,384]{2,1,0:T(8,128)(2,1)S(1)}, u32[]{:S(2)}, u32[]{:S(2)}) %collective-permute-start.8) | collective-permute-done | bytes 196640 | tf_op jit(solution)/shard_map/ppermute | solution.py:250
  20.1 2.4 %collective-permute-start.2 = (bf16[4,128,384]{2,1,0:T(8,128)(2,1)S(1)}, bf16[4,128,384]{2,1,0:T(8,128)(2,1)S(1)}, u32[]{:S(2)}, u32[]{:S(2)}) collective-permute-start(bf16[4,128,384]{2,1,0:T(8,128)(2,1)S(1)} %get-tuple-element.29), channel_id=1, source_target_pairs={{0,24},{1,25},{2,26},{3,27},{4,28},{5,29},{6,30},{7,31},{8,16},{9,... | collective-permute-start | bytes 1179656 | tf_op jit(solution)/shard_map/ppermute | solution.py:250
  22.6 2.1 %collective-permute-done.9.refs_14_ = bf16[2,128,384]{2,1,0:T(8,128)(2,1)S(1)} collective-permute-done((bf16[2,128,384]{2,1,0:T(8,128)(2,1)S(1)}, bf16[2,128,384]{2,1,0:T(8,128)(2,1)S(1)}, u32[]{:S(2)}, u32[]{:S(2)}) %collective-permute-start.9) | collective-permute-done | bytes 196640 | tf_op jit(solution)/shard_map/ppermute | solution.py:250
  24.6 3.9 %collective-permute-done.10.refs_15_ = bf16[2,128,384]{2,1,0:T(8,128)(2,1)} collective-permute-done((bf16[2,128,384]{2,1,0:T(8,128)(2,1)S(1)}, bf16[2,128,384]{2,1,0:T(8,128)(2,1)}, u32[]{:S(2)}, u32[]{:S(2)}) %collective-permute-start.10) | collective-permute-done | bytes 196640 | tf_op jit(solution)/shard_map/ppermute | solution.py:250
  31.6 10.0 %collective-permute-done.1.refs_6_ = bf16[4,128,384]{2,1,0:T(8,128)(2,1)S(1)} collective-permute-done((bf16[4,128,384]{2,1,0:T(8,128)(2,1)S(1)}, bf16[4,128,384]{2,1,0:T(8,128)(2,1)S(1)}, u32[]{:S(2)}, u32[]{:S(2)}) %collective-permute-start.1) | collective-permute-done | bytes 393248 | tf_op jit(solution)/shard_map/ppermute | solution.py:250
  42.8 1.8 %copy.12 = f32[1000,12]{1,0:T(8,128)} copy(f32[1000,12]{0,1:T(8,128)} %param.15) | data formatting | bytes 96000 | tf_op args[7]
  45.2 1.7 %gather_fusion = f32[8,12]{1,0:T(8,128)S(1)} fusion(f32[1000,12]{1,0:T(8,128)} %copy.12, s32[1024]{0:T(1024)} %pad_clamp_fusion), kind=kCustom, calls=%fused_computation | custom fusion | bytes 800 | tf_op jit(solution)/shard_map/gather | solution.py:270
  50.7 19.5 %attention.1 = (bf16[2,128,384]{2,1,0:T(8,128)(2,1)S(1)}, bf16[2,128,384]{2,1,0:T(8,128)(2,1)S(1)}, bf16[2,128,384]{2,1,0:T(8,128)(2,1)S(1)}, bf16[2,128,384]{2,...) custom-call(s32[3]{0:T(128)S(1)} %pad_add_fusion.pos_ref.refs_0_, ...), custom_call_target="tpu_custom_call" | custom-call | tf_op jit(solution)/shard_map/attention/pallas_call | solution.py:201
  70.2 1.5 %collective-permute-start.15 = (bf16[2,128,384]{2,1,0:T(8,128)(2,1)S(1)}, bf16[2,128,384]{2,1,0:T(8,128)(2,1)S(1)}, u32[]{:S(2)}, u32[]{:S(2)}) collective-permute-start(bf16[2,128,384]{2,1,0:T(8,128)(2,1)S(1)} %get-tuple-element.35), channel_id=1, source_target_pairs={{0,8},{1,9},{2,10},{3,11},{4,12},{5,13},{6,14},{7,15},{8,0},{9,1},... | collective-permute-start | bytes 589832 | tf_op jit(solution)/shard_map/ppermute | solution.py:250
  71.7 1.5 %collective-permute-start.16 = (bf16[2,128,384]{2,1,0:T(8,128)(2,1)S(1)}, bf16[2,128,384]{2,1,0:T(8,128)(2,1)S(1)}, u32[]{:S(2)}, u32[]{:S(2)}) collective-permute-start(bf16[2,128,384]{2,1,0:T(8,128)(2,1)S(1)} %get-tuple-element.36), channel_id=1, source_target_pairs={{0,16},{1,17},{2,18},{3,19},{4,20},{5,21},{6,22},{7,23},{8,24},{9,... | collective-permute-start | bytes 589832 | tf_op jit(solution)/shard_map/ppermute | solution.py:250
  75.6 1.6 %collective-permute-start.19 = (bf16[2,128,384]{2,1,0:T(8,128)(2,1)S(1)}, bf16[2,128,384]{2,1,0:T(8,128)(2,1)S(1)}, u32[]{:S(2)}, u32[]{:S(2)}) collective-permute-start(bf16[2,128,384]{2,1,0:T(8,128)(2,1)S(1)} %get-tuple-element.41), channel_id=1, source_target_pairs={{0,8},{1,9},{2,10},{3,11},{4,12},{5,13},{6,14},{7,15},{8,0},{9,1},... | collective-permute-start | bytes 589832 | tf_op jit(solution)/shard_map/ppermute | solution.py:250
  77.2 1.5 %collective-permute-start.20 = (bf16[2,128,384]{2,1,0:T(8,128)(2,1)S(1)}, bf16[2,128,384]{2,1,0:T(8,128)(2,1)S(1)}, u32[]{:S(2)}, u32[]{:S(2)}) collective-permute-start(bf16[2,128,384]{2,1,0:T(8,128)(2,1)S(1)} %get-tuple-element.42), channel_id=1, source_target_pairs={{0,16},{1,17},{2,18},{3,19},{4,20},{5,21},{6,22},{7,23},{8,24},{9,... | collective-permute-start | bytes 589832 | tf_op jit(solution)/shard_map/ppermute | solution.py:250
  78.7 1.7 %collective-permute-start.21 = (bf16[2,128,384]{2,1,0:T(8,128)(2,1)S(1)}, bf16[2,128,384]{2,1,0:T(8,128)(2,1)S(1)}, u32[]{:S(2)}, u32[]{:S(2)}) collective-permute-start(bf16[2,128,384]{2,1,0:T(8,128)(2,1)S(1)} %get-tuple-element.43), channel_id=1, source_target_pairs={{0,24},{1,25},{2,26},{3,27},{4,28},{5,29},{6,30},{7,31},{8,16},{9,... | collective-permute-start | bytes 589832 | tf_op jit(solution)/shard_map/ppermute | solution.py:250
  80.4 2.6 %collective-permute-done.16.refs_2_ = bf16[2,128,384]{2,1,0:T(8,128)(2,1)S(1)} collective-permute-done((bf16[2,128,384]{2,1,0:T(8,128)(2,1)S(1)}, bf16[2,128,384]{2,1,0:T(8,128)(2,1)S(1)}, u32[]{:S(2)}, u32[]{:S(2)}) %collective-permute-start.16) | collective-permute-done | bytes 196640 | tf_op jit(solution)/shard_map/ppermute | solution.py:250
  83.5 3.4 %collective-permute-start.23 = (bf16[2,128,384]{2,1,0:T(8,128)(2,1)S(1)}, bf16[2,128,384]{2,1,0:T(8,128)(2,1)S(1)}, u32[]{:S(2)}, u32[]{:S(2)}) collective-permute-start(bf16[2,128,384]{2,1,0:T(8,128)(2,1)S(1)} %get-tuple-element.45), channel_id=1, source_target_pairs={{0,9},{1,10},{2,11},{3,8},{4,13},{5,14},{6,15},{7,12},{8,1},{9,2},... | collective-permute-start | bytes 589832 | tf_op jit(solution)/shard_map/ppermute | solution.py:250
  86.9 4.7 %collective-permute-start.24 = (bf16[2,128,384]{2,1,0:T(8,128)(2,1)S(1)}, bf16[2,128,384]{2,1,0:T(8,128)(2,1)S(1)}, u32[]{:S(2)}, u32[]{:S(2)}) collective-permute-start(bf16[2,128,384]{2,1,0:T(8,128)(2,1)S(1)} %get-tuple-element.46), channel_id=1, source_target_pairs={{0,17},{1,18},{2,19},{3,16},{4,21},{5,22},{6,23},{7,20},{8,25},{9,... | collective-permute-start | bytes 589832 | tf_op jit(solution)/shard_map/ppermute | solution.py:250
  91.6 1.6 %collective-permute-start.25 = (bf16[2,128,384]{2,1,0:T(8,128)(2,1)S(1)}, bf16[2,128,384]{2,1,0:T(8,128)(2,1)S(1)}, u32[]{:S(2)}, u32[]{:S(2)}) collective-permute-start(bf16[2,128,384]{2,1,0:T(8,128)(2,1)S(1)} %get-tuple-element.47), channel_id=1, source_target_pairs={{0,25},{1,26},{2,27},{3,24},{4,29},{5,30},{6,31},{7,28},{8,17},{9,... | collective-permute-start | bytes 589832 | tf_op jit(solution)/shard_map/ppermute | solution.py:250
  93.2 2.1 %collective-permute-done.22.refs_8_ = bf16[2,128,384]{2,1,0:T(8,128)(2,1)S(1)} collective-permute-done((bf16[2,128,384]{2,1,0:T(8,128)(2,1)S(1)}, bf16[2,128,384]{2,1,0:T(8,128)(2,1)S(1)}, u32[]{:S(2)}, u32[]{:S(2)}) %collective-permute-start.22) | collective-permute-done | bytes 196640 | tf_op jit(solution)/shard_map/ppermute | solution.py:250
  95.3 1.8 %collective-permute-done.23.refs_9_ = bf16[2,128,384]{2,1,0:T(8,128)(2,1)S(1)} collective-permute-done((bf16[2,128,384]{2,1,0:T(8,128)(2,1)S(1)}, bf16[2,128,384]{2,1,0:T(8,128)(2,1)S(1)}, u32[]{:S(2)}, u32[]{:S(2)}) %collective-permute-start.23) | collective-permute-done | bytes 196640 | tf_op jit(solution)/shard_map/ppermute | solution.py:250
  97.1 9.2 %collective-permute-done.24.refs_10_ = bf16[2,128,384]{2,1,0:T(8,128)(2,1)S(1)} collective-permute-done((bf16[2,128,384]{2,1,0:T(8,128)(2,1)S(1)}, bf16[2,128,384]{2,1,0:T(8,128)(2,1)S(1)}, u32[]{:S(2)}, u32[]{:S(2)}) %collective-permute-start.24) | collective-permute-done | bytes 196640 | tf_op jit(solution)/shard_map/ppermute | solution.py:250
  106.6 1.8 %unpack.1 = (bf16[128,1536]{1,0:T(8,128)(2,1)}, bf16[128,1536]{1,0:T(8,128)(2,1)}, bf16[128,1536]{1,0:T(8,128)(2,1)}, bf16[128,1536]{1,0:T(8,128)(2,1)}) custom-call(s32[3]{0:T(128)S(1)} %pad_add_fusion.pos_ref.refs_0_, bf16[2,128,384]{2,1,0:T(8,128)(2,1)S(1)} %get-tuple-element.34.refs_0_, bf16[2,128,384]{2,1,0:T(8,128)(2,1)S(1)} %collective-permute-done.15.refs_1_, ...), custom_call_target="tpu_custom_call" | custom-call | tf_op jit(solution)/shard_map/unpack/pallas_call | solution.py:291
  (69 shorter events, 20.1 us)
Async XLA Ops:
  5.5 10.4 %collective-permute-start.7 = (bf16[2,128,384]{2,1,0:T(8,128)(2,1)S(1)}, bf16[2,128,384]{2,1,0:T(8,128)(2,1)S(1)}, u32[]{:S(2)}, u32[]{:S(2)}) collective-permute-start(bf16[2,128,384]{2,1,0:T(8,128)(2,1)S(1)} %get-tuple-element.30), channel_id=1, source_target_pairs={{0,3},{1,0},{2,1},{3,2},{4,7},{5,4},{6,5},{7,6},{8,11},{9,8},{10,9... | collective-permute-start | bytes 589832 | tf_op jit(solution)/shard_map/ppermute | solution.py:250
  10.6 9.5 %collective-permute-start.8 = (bf16[2,128,384]{2,1,0:T(8,128)(2,1)S(1)}, bf16[2,128,384]{2,1,0:T(8,128)(2,1)S(1)}, u32[]{:S(2)}, u32[]{:S(2)}) collective-permute-start(bf16[2,128,384]{2,1,0:T(8,128)(2,1)S(1)} %get-tuple-element.31), channel_id=1, source_target_pairs={{0,11},{1,8},{2,9},{3,10},{4,15},{5,12},{6,13},{7,14},{8,3},{9,0},... | collective-permute-start | bytes 589832 | tf_op jit(solution)/shard_map/ppermute | solution.py:250
  12.0 12.6 %collective-permute-start.9 = (bf16[2,128,384]{2,1,0:T(8,128)(2,1)S(1)}, bf16[2,128,384]{2,1,0:T(8,128)(2,1)S(1)}, u32[]{:S(2)}, u32[]{:S(2)}) collective-permute-start(bf16[2,128,384]{2,1,0:T(8,128)(2,1)S(1)} %get-tuple-element.32), channel_id=1, source_target_pairs={{0,19},{1,16},{2,17},{3,18},{4,23},{5,20},{6,21},{7,22},{8,27},{9,... | collective-permute-start | bytes 589832 | tf_op jit(solution)/shard_map/ppermute | solution.py:250
  13.4 15.1 %collective-permute-start.10 = (bf16[2,128,384]{2,1,0:T(8,128)(2,1)S(1)}, bf16[2,128,384]{2,1,0:T(8,128)(2,1)}, u32[]{:S(2)}, u32[]{:S(2)}) collective-permute-start(bf16[2,128,384]{2,1,0:T(8,128)(2,1)S(1)} %get-tuple-element.33), channel_id=1, source_target_pairs={{0,27},{1,24},{2,25},{3,26},{4,31},{5,28},{6,29},{7,30},{8,19},{9,... | collective-permute-start | bytes 589832 | tf_op jit(solution)/shard_map/ppermute | solution.py:250
  13.4 18.1 %collective-permute-start = (bf16[4,128,384]{2,1,0:T(8,128)(2,1)S(1)}, bf16[4,128,384]{2,1,0:T(8,128)(2,1)S(1)}, u32[]{:S(2)}, u32[]{:S(2)}) collective-permute-start(bf16[4,128,384]{2,1,0:T(8,128)(2,1)S(1)} %get-tuple-element.27), channel_id=1, source_target_pairs={{0,8},{1,9},{2,10},{3,11},{4,12},{5,13},{6,14},{7,15},{8,0},{9,1},... | collective-permute-start | bytes 1179656 | tf_op jit(solution)/shard_map/ppermute | solution.py:250
  15.9 25.7 %collective-permute-start.1 = (bf16[4,128,384]{2,1,0:T(8,128)(2,1)S(1)}, bf16[4,128,384]{2,1,0:T(8,128)(2,1)S(1)}, u32[]{:S(2)}, u32[]{:S(2)}) collective-permute-start(bf16[4,128,384]{2,1,0:T(8,128)(2,1)S(1)} %get-tuple-element.28), channel_id=1, source_target_pairs={{0,16},{1,17},{2,18},{3,19},{4,20},{5,21},{6,22},{7,23},{8,24},{9,... | collective-permute-start | bytes 1179656 | tf_op jit(solution)/shard_map/ppermute | solution.py:250
  20.1 21.5 %collective-permute-start.2 = (bf16[4,128,384]{2,1,0:T(8,128)(2,1)S(1)}, bf16[4,128,384]{2,1,0:T(8,128)(2,1)S(1)}, u32[]{:S(2)}, u32[]{:S(2)}) collective-permute-start(bf16[4,128,384]{2,1,0:T(8,128)(2,1)S(1)} %get-tuple-element.29), channel_id=1, source_target_pairs={{0,24},{1,25},{2,26},{3,27},{4,28},{5,29},{6,30},{7,31},{8,16},{9,... | collective-permute-start | bytes 1179656 | tf_op jit(solution)/shard_map/ppermute | solution.py:250
  24.6 3.9 %collective-permute-start.11 = (bf16[2,128,384]{2,1,0:T(8,128)(2,1)S(1)}, bf16[2,128,384]{2,1,0:T(8,128)(2,1)S(1)}, u32[]{:S(2)}, u32[]{:S(2)}) collective-permute-start(bf16[2,128,384]{2,1,0:T(8,128)(2,1)S(1)} %collective-permute-done.7.refs_12_), channel_id=1, source_target_pairs={{0,4},{4,0},{8,12},{12,8},{16,20},{20,16},{24,28},{28,24},{1,5},{5... | collective-permute-start | bytes 589832 | tf_op jit(solution)/shard_map/ppermute | solution.py:254
  29.2 12.9 %collective-permute-start.13 = (bf16[2,128,384]{2,1,0:T(8,128)(2,1)S(1)}, bf16[2,128,384]{2,1,0:T(8,128)(2,1)S(1)}, u32[]{:S(2)}, u32[]{:S(2)}) collective-permute-start(bf16[2,128,384]{2,1,0:T(8,128)(2,1)S(1)} %collective-permute-done.9.refs_14_), channel_id=1, source_target_pairs={{0,4},{4,0},{8,12},{12,8},{16,20},{20,16},{24,28},{28,24},{1,5},{5... | collective-permute-start | bytes 589832 | tf_op jit(solution)/shard_map/ppermute | solution.py:254
  31.1 15.9 %collective-permute-start.3 = (bf16[4,128,384]{2,1,0:T(8,128)(2,1)S(1)}, bf16[4,128,384]{2,1,0:T(8,128)(2,1)S(1)}, u32[]{:S(2)}, u32[]{:S(2)}) collective-permute-start(bf16[4,128,384]{2,1,0:T(8,128)(2,1)S(1)} %get-tuple-element.26.refs_4_), channel_id=1, source_target_pairs={{0,4},{4,0},{8,12},{12,8},{16,20},{20,16},{24,28},{28,24},{1,5},{5... | collective-permute-start | bytes 1179656 | tf_op jit(solution)/shard_map/ppermute | solution.py:254
  31.5 15.5 %collective-permute-start.4 = (bf16[4,128,384]{2,1,0:T(8,128)(2,1)S(1)}, bf16[4,128,384]{2,1,0:T(8,128)(2,1)S(1)}, u32[]{:S(2)}, u32[]{:S(2)}) collective-permute-start(bf16[4,128,384]{2,1,0:T(8,128)(2,1)S(1)} %collective-permute-done.refs_5_), channel_id=1, source_target_pairs={{0,4},{4,0},{8,12},{12,8},{16,20},{20,16},{24,28},{28,24},{1,5},{5... | collective-permute-start | bytes 1179656 | tf_op jit(solution)/shard_map/ppermute | solution.py:254
  41.6 5.4 %collective-permute-start.5 = (bf16[4,128,384]{2,1,0:T(8,128)(2,1)S(1)}, bf16[4,128,384]{2,1,0:T(8,128)(2,1)S(1)}, u32[]{:S(2)}, u32[]{:S(2)}) collective-permute-start(bf16[4,128,384]{2,1,0:T(8,128)(2,1)S(1)} %collective-permute-done.1.refs_6_), channel_id=1, source_target_pairs={{0,4},{4,0},{8,12},{12,8},{16,20},{20,16},{24,28},{28,24},{1,5},{5... | collective-permute-start | bytes 1179656 | tf_op jit(solution)/shard_map/ppermute | solution.py:254
  41.6 5.4 %collective-permute-start.6 = (bf16[4,128,384]{2,1,0:T(8,128)(2,1)S(1)}, bf16[4,128,384]{2,1,0:T(8,128)(2,1)S(1)}, u32[]{:S(2)}, u32[]{:S(2)}) collective-permute-start(bf16[4,128,384]{2,1,0:T(8,128)(2,1)S(1)} %collective-permute-done.2.refs_7_), channel_id=1, source_target_pairs={{0,4},{4,0},{8,12},{12,8},{16,20},{20,16},{24,28},{28,24},{1,5},{5... | collective-permute-start | bytes 1179656 | tf_op jit(solution)/shard_map/ppermute | solution.py:254
  42.8 4.2 %collective-permute-start.14 = (bf16[2,128,384]{2,1,0:T(8,128)(2,1)}, bf16[2,128,384]{2,1,0:T(8,128)(2,1)}, u32[]{:S(2)}, u32[]{:S(2)}) collective-permute-start(bf16[2,128,384]{2,1,0:T(8,128)(2,1)} %collective-permute-done.10.refs_15_), channel_id=1, source_target_pairs={{0,4},{4,0},{8,12},{12,8},{16,20},{20,16},{24,28},{28,24},{1,5},{5... | collective-permute-start | bytes 589832 | tf_op jit(solution)/shard_map/ppermute | solution.py:254
  70.2 8.5 %collective-permute-start.15 = (bf16[2,128,384]{2,1,0:T(8,128)(2,1)S(1)}, bf16[2,128,384]{2,1,0:T(8,128)(2,1)S(1)}, u32[]{:S(2)}, u32[]{:S(2)}) collective-permute-start(bf16[2,128,384]{2,1,0:T(8,128)(2,1)S(1)} %get-tuple-element.35), channel_id=1, source_target_pairs={{0,8},{1,9},{2,10},{3,11},{4,12},{5,13},{6,14},{7,15},{8,0},{9,1},... | collective-permute-start | bytes 589832 | tf_op jit(solution)/shard_map/ppermute | solution.py:250
  71.7 11.2 %collective-permute-start.16 = (bf16[2,128,384]{2,1,0:T(8,128)(2,1)S(1)}, bf16[2,128,384]{2,1,0:T(8,128)(2,1)S(1)}, u32[]{:S(2)}, u32[]{:S(2)}) collective-permute-start(bf16[2,128,384]{2,1,0:T(8,128)(2,1)S(1)} %get-tuple-element.36), channel_id=1, source_target_pairs={{0,16},{1,17},{2,18},{3,19},{4,20},{5,21},{6,22},{7,23},{8,24},{9,... | collective-permute-start | bytes 589832 | tf_op jit(solution)/shard_map/ppermute | solution.py:250
  73.2 10.2 %collective-permute-start.17 = (bf16[2,128,384]{2,1,0:T(8,128)(2,1)S(1)}, bf16[2,128,384]{2,1,0:T(8,128)(2,1)S(1)}, u32[]{:S(2)}, u32[]{:S(2)}) collective-permute-start(bf16[2,128,384]{2,1,0:T(8,128)(2,1)S(1)} %get-tuple-element.37), channel_id=1, source_target_pairs={{0,24},{1,25},{2,26},{3,27},{4,28},{5,29},{6,30},{7,31},{8,16},{9,... | collective-permute-start | bytes 589832 | tf_op jit(solution)/shard_map/ppermute | solution.py:250
  75.6 11.3 %collective-permute-start.19 = (bf16[2,128,384]{2,1,0:T(8,128)(2,1)S(1)}, bf16[2,128,384]{2,1,0:T(8,128)(2,1)S(1)}, u32[]{:S(2)}, u32[]{:S(2)}) collective-permute-start(bf16[2,128,384]{2,1,0:T(8,128)(2,1)S(1)} %get-tuple-element.41), channel_id=1, source_target_pairs={{0,8},{1,9},{2,10},{3,11},{4,12},{5,13},{6,14},{7,15},{8,0},{9,1},... | collective-permute-start | bytes 589832 | tf_op jit(solution)/shard_map/ppermute | solution.py:250
  77.2 14.4 %collective-permute-start.20 = (bf16[2,128,384]{2,1,0:T(8,128)(2,1)S(1)}, bf16[2,128,384]{2,1,0:T(8,128)(2,1)S(1)}, u32[]{:S(2)}, u32[]{:S(2)}) collective-permute-start(bf16[2,128,384]{2,1,0:T(8,128)(2,1)S(1)} %get-tuple-element.42), channel_id=1, source_target_pairs={{0,16},{1,17},{2,18},{3,19},{4,20},{5,21},{6,22},{7,23},{8,24},{9,... | collective-permute-start | bytes 589832 | tf_op jit(solution)/shard_map/ppermute | solution.py:250
  78.7 14.5 %collective-permute-start.21 = (bf16[2,128,384]{2,1,0:T(8,128)(2,1)S(1)}, bf16[2,128,384]{2,1,0:T(8,128)(2,1)S(1)}, u32[]{:S(2)}, u32[]{:S(2)}) collective-permute-start(bf16[2,128,384]{2,1,0:T(8,128)(2,1)S(1)} %get-tuple-element.43), channel_id=1, source_target_pairs={{0,24},{1,25},{2,26},{3,27},{4,28},{5,29},{6,30},{7,31},{8,16},{9,... | collective-permute-start | bytes 589832 | tf_op jit(solution)/shard_map/ppermute | solution.py:250
  82.9 12.3 %collective-permute-start.22 = (bf16[2,128,384]{2,1,0:T(8,128)(2,1)S(1)}, bf16[2,128,384]{2,1,0:T(8,128)(2,1)S(1)}, u32[]{:S(2)}, u32[]{:S(2)}) collective-permute-start(bf16[2,128,384]{2,1,0:T(8,128)(2,1)S(1)} %get-tuple-element.44), channel_id=1, source_target_pairs={{0,1},{1,2},{2,3},{3,0},{4,5},{5,6},{6,7},{7,4},{8,9},{9,10},{10,1... | collective-permute-start | bytes 589832 | tf_op jit(solution)/shard_map/ppermute | solution.py:250
  83.5 13.6 %collective-permute-start.23 = (bf16[2,128,384]{2,1,0:T(8,128)(2,1)S(1)}, bf16[2,128,384]{2,1,0:T(8,128)(2,1)S(1)}, u32[]{:S(2)}, u32[]{:S(2)}) collective-permute-start(bf16[2,128,384]{2,1,0:T(8,128)(2,1)S(1)} %get-tuple-element.45), channel_id=1, source_target_pairs={{0,9},{1,10},{2,11},{3,8},{4,13},{5,14},{6,15},{7,12},{8,1},{9,2},... | collective-permute-start | bytes 589832 | tf_op jit(solution)/shard_map/ppermute | solution.py:250
  86.9 19.3 %collective-permute-start.24 = (bf16[2,128,384]{2,1,0:T(8,128)(2,1)S(1)}, bf16[2,128,384]{2,1,0:T(8,128)(2,1)S(1)}, u32[]{:S(2)}, u32[]{:S(2)}) collective-permute-start(bf16[2,128,384]{2,1,0:T(8,128)(2,1)S(1)} %get-tuple-element.46), channel_id=1, source_target_pairs={{0,17},{1,18},{2,19},{3,16},{4,21},{5,22},{6,23},{7,20},{8,25},{9,... | collective-permute-start | bytes 589832 | tf_op jit(solution)/shard_map/ppermute | solution.py:250
  91.6 15.0 %collective-permute-start.25 = (bf16[2,128,384]{2,1,0:T(8,128)(2,1)S(1)}, bf16[2,128,384]{2,1,0:T(8,128)(2,1)S(1)}, u32[]{:S(2)}, u32[]{:S(2)}) collective-permute-start(bf16[2,128,384]{2,1,0:T(8,128)(2,1)S(1)} %get-tuple-element.47), channel_id=1, source_target_pairs={{0,25},{1,26},{2,27},{3,24},{4,29},{5,30},{6,31},{7,28},{8,17},{9,... | collective-permute-start | bytes 589832 | tf_op jit(solution)/shard_map/ppermute | solution.py:250
  (18 other events, 152.2 us)

commit v3 on v2

--- a/solution.py
+++ b/solution.py
@@ -31,32 +31,37 @@
     return count
 
 
-def pack_kernel(shards, width, pos_ref, q_ref, g_ref, k_ref, v_ref, *outs):
+def pack_kernel(shards, width, pos_ref, *refs):
+    sources, outs, held, sems = refs[:4], refs[4:-2], refs[-2], refs[-1]
     shard = pos_ref[0]
-    for hop in range(shards):
-        lane = pl.multiple_of((shard ^ hop) * width, 128)
-        full, pair = outs[hop], outs[shards + hop]
-        full[0] = q_ref[:, pl.ds(lane, width)]
-        full[1] = g_ref[:, pl.ds(lane, width)]
-        k = k_ref[:, pl.ds(lane, width)]
-        v = v_ref[:, pl.ds(lane, width)]
-        full[2] = k
-        full[3] = v
-        pair[0] = k
-        pair[1] = v
+    half = held.shape[1] // 2
+    copies = []
+    for i, src in enumerate(sources):
+        for j in range(2):
+            rows = pl.ds(j * half, half)
+            copy = pltpu.make_async_copy(src.at[rows], held.at[i, rows], sems.at[i, j])
+            copy.start()
+            copies.append(copy)
+    for i in (2, 3, 0, 1):
+        copies[2 * i].wait()
+        copies[2 * i + 1].wait()
+        for hop in range(shards):
+            part = held[i, :, pl.ds(pl.multiple_of((shard ^ hop) * width, 128), width)]
+            outs[hop][i] = part
+            if i >= 2:
+                outs[shards + hop][i - 2] = part
 
 
 def attention_kernel(shards, replicas, tiles, own_heads, batch, inv_root, *refs):
     slots = shards * replicas
-    pos_ref, span_ref, live_ref, bias_ref = refs[:4]
-    full = refs[4 : 4 + slots]
-    ahead = refs[4 + slots : 4 + 2 * slots]
-    outs = refs[4 + 2 * slots : 4 + 2 * slots + shards + replicas]
+    pos_ref, span_ref, live_ref, level_ref, table_ref = refs[:5]
+    full, ahead = refs[5 : 5 + slots], refs[5 + slots : 5 + 2 * slots]
+    outs = refs[5 + 2 * slots : 5 + 2 * slots + shards + replicas]
     rows_out, sums_out = outs[:shards], outs[shards:]
-    kv, kt, vt, acc, score, dprob, both, ot, dqt = refs[4 + 2 * slots + shards + replicas :]
+    kv, kt, vt, acc, score, dprob, both, ot, dqt, bias = refs[5 + 2 * slots + shards + replicas :]
     tok, width = kv.shape[2] // 2, kv.shape[3] // 2
     shard, replica, tile = pos_ref[0], pos_ref[1], pos_ref[2]
-    first = shard * own_heads + pl.program_id(0) * batch
+    first = shard * own_heads + (0 if batch == own_heads else pl.program_id(0) * batch)
     heads = range(batch)
     scale = inv_root * LOG2E
 
@@ -78,6 +83,13 @@
                     kv[h, span, part, width:] = v
                     kt[h, span, :, part] = k.T
                     vt[h, span, :, part] = v.T
+    table = table_ref[...]
+    level_ids = lax.broadcasted_iota(jnp.int32, table.shape, 1)
+    for span in range(slots):
+        column = jnp.sum(
+            jnp.where(level_ids == level_ref[span], table, 0.0), axis=1, keepdims=True
+        )
+        bias[span] = jnp.broadcast_to(column * LOG2E, bias.shape[1:])
     acc[...] = jnp.zeros_like(acc)
     both[...] = jnp.zeros_like(both)
 
@@ -95,7 +107,7 @@
             new = []
             for h in heads:
                 sd = lax.dot_general(kv[h, i, :rows, :], both[h], NT, preferred_element_type=F32)
-                s = sd[:, :tok] * scale + bias_ref[i, first + h] * LOG2E
+                s = sd[:, :tok] * scale + bias[i, pl.ds(first + h, 1), :]
                 score[h, i, :rows, :] = s
                 dprob[h, i, :rows, :] = sd[:, tok:]
                 new.append(jnp.maximum(peaks[h], fold(jnp.max, s)))
@@ -187,26 +199,30 @@
         dv_ref[:, lanes] = (sums[hop][1].astype(F32) + ahead[hop][1].astype(F32)).astype(BF16)
 
 
-def attend(sizes, pos, span_of_group, next_live, bias, full, ahead):
+def attend(sizes, pos, span_of_group, next_live, noise_level, bias_table, full, ahead):
     shards, replicas, tiles, own_heads, width, tok = sizes
     groups = shards * replicas
     batch = own_heads if groups <= 8 else 1
     cols, step = own_heads * width, batch * width
     shape = jax.ShapeDtypeStruct
 
-    def head_block(count):
-        return pl.BlockSpec((count, tok, step), lambda h: (0, 0, h))
-
-    stacked = pl.BlockSpec((shards, 4, tok, step), lambda h: (0, 0, 0, h))
+    if batch == own_heads:
+        grid = ()
+        narrow = wide = stacked = whole(VMEM)
+    else:
+        grid = (own_heads // batch,)
+        narrow = pl.BlockSpec((2, tok, step), lambda h: (0, 0, h))
+        wide = pl.BlockSpec((4, tok, step), lambda h: (0, 0, h))
+        stacked = pl.BlockSpec((shards, 4, tok, step), lambda h: (0, 0, 0, h))
     return pl.pallas_call(
         functools.partial(
             attention_kernel, shards, replicas, tiles, own_heads, batch, 1.0 / math.sqrt(width)
         ),
-        grid=(own_heads // batch,),
+        grid=grid,
         out_shape=[shape((2, tok, cols), BF16)] * shards
         + [shape((shards, 4, tok, cols), BF16)] * replicas,
-        in_specs=[whole(SMEM)] * 4 + [head_block(4)] * groups + [head_block(2)] * groups,
-        out_specs=[head_block(2)] * shards + [stacked] * replicas,
+        in_specs=[whole(SMEM)] * 4 + [whole(VMEM)] + [wide] * groups + [narrow] * groups,
+        out_specs=[narrow] * shards + [stacked] * replicas,
         scratch_shapes=[
             VMEM((batch, groups, 2 * tok, 2 * width), BF16),
             VMEM((batch, groups, width, 2 * tok), BF16),
@@ -217,10 +233,11 @@
             VMEM((batch, 2 * tok, 2 * width), BF16),
             VMEM((batch, width, tok), F32),
             VMEM((batch, width, tok), F32),
+            VMEM((groups, bias_table.shape[0], tok), F32),
         ],
-        compiler_params=params(48),
+        compiler_params=params(30 if batch == own_heads else 48),
         name="attention",
-    )(pos, span_of_group, next_live, bias, *full, *ahead)
+    )(pos, span_of_group, next_live, noise_level, bias_table, *full, *ahead)
 
 
 def per_device(queries, keys, values, grad_out, span_of_group, noise_level, next_live, level_bias):
@@ -256,22 +273,22 @@
     packed = pl.pallas_call(
         functools.partial(pack_kernel, shards, cols),
         out_shape=[shape((4, tok, cols), BF16)] * shards + [shape((2, tok, cols), BF16)] * shards,
-        in_specs=[whole(SMEM)] + [whole(VMEM)] * 4,
+        in_specs=[whole(SMEM)] + [whole(pltpu.HBM)] * 4,
         out_specs=[whole(VMEM)] * (2 * shards),
-        compiler_params=params(32),
+        scratch_shapes=[VMEM((4, tok, model), BF16), pltpu.SemaphoreType.DMA((4, 2))],
+        compiler_params=params(8),
         name="pack",
-    )(pos, queries, grad_out, keys, values)
+    )(pos, *(pltpu.with_memory_space_constraint(x, pltpu.HBM) for x in (queries, grad_out, keys, values)))
     full = [to_shard(packed[hop], hop, 0) for hop in range(shards)]
     ahead = [to_shard(packed[shards + hop], hop, -1) for hop in range(shards)]
     full_all, ahead_all = list(full), list(ahead)
     for turn in range(1, replicas):
         full_all += [to_replica(x, turn) for x in full]
         ahead_all += [to_replica(x, turn) for x in ahead]
-    bias = level_bias.at[noise_level].get(mode="promise_in_bounds")
 
     results = attend(
         (shards, replicas, tiles, own_heads, width, tok),
-        pos, span_of_group, next_live, bias, full_all, ahead_all,
+        pos, span_of_group, next_live, noise_level, level_bias.T, full_all, ahead_all,
     )
     rows, sums = results[:shards], results[shards:]
     rows_home = [to_shard(rows[hop], hop, 0) for hop in range(shards)]
@@ -283,7 +300,7 @@
         out_shape=[shape((2, tok, cols), BF16)] * (2 * shards),
         in_specs=[whole(VMEM)] * replicas,
         out_specs=[whole(VMEM)] * (2 * shards),
-        compiler_params=params(48),
+        compiler_params=params(8),
         name="merge",
     )(*parts)
     sums_home = [to_shard(merged[hop], hop, 0) for hop in range(shards)]
@@ -293,7 +310,7 @@
         out_shape=[shape((tok, model), BF16)] * 4,
         in_specs=[whole(SMEM)] + [whole(VMEM)] * (3 * shards),
         out_specs=[whole(VMEM)] * 4,
-        compiler_params=params(32),
+        compiler_params=params(8),
         name="unpack",
     )(pos, *rows_home, *sums_home, *ahead_home)
 

time: 110 us -> 95.2 us (0.87); the launches traced: 108 us -> 94.9 us
  local copies, waits for them, and re-layouts: 15.4 us -> 0.02 us
  starting transfers between devices: 33.3 us -> 37.5 us
  Pallas kernels: 22.4 us -> 18.5 us
  waiting for transfers between devices: 35.9 us -> 38 us
    unnamed x33 -> x8, local copies, waits for them, and re-layouts: 13.6 us -> 0.02 us
    pallas_call x1, Pallas kernels: 19.5 us -> 14.2 us  [attend(): pl.pallas_call(functools.partial(attention_kernel, shards, replicas, tile...]
    ppermute x9, waiting for transfers between devices: 0.15 us -> 2.92 us  [to_replica(): return lax.ppermute(x, 'tm', pairs)]
    ppermute x9, starting transfers between devices: 1.09 us -> 3.58 us  [to_replica(): return lax.ppermute(x, 'tm', pairs)]
    ppermute x17, starting transfers between devices: 32.2 us -> 33.9 us  [to_shard(): return lax.ppermute(x, ('tm', 'tile'), pairs)]
    gather x1 -> x0, local copies, waits for them, and re-layouts: 1.71 us -> none  [per_device(): bias = level_bias.at[noise_level].get(mode='promise_in_bounds')]
    pallas_call x1, Pallas kernels: 0.75 us -> 2.21 us  [per_device(): pl.pallas_call(functools.partial(pack_kernel, shards, cols), out_shape=[s...]
  transfers between devices with their start and end apart: 26 -> 26, of which waited for: 12 -> 13; matrix products, arithmetic and copies ran while one was open for 4% -> 0% of each run, Pallas kernels for 0% -> 0%
where the time goes in v3:
time: 95.2 us; the launch traced here: 94.9 us
  waiting for transfers between devices  38 us (40%)
  starting transfers between devices  37.5 us (39%)
  Pallas kernels  18.5 us (19%)
    ppermute x17, waiting for transfers between devices, to_shard(): return lax.ppermute(x, ('tm', 'tile'), pairs)  35.1 us
    ppermute x17, starting transfers between devices, to_shard(): return lax.ppermute(x, ('tm', 'tile'), pairs)  33.9 us
    pallas_call x1, Pallas kernels, attend(): pl.pallas_call(functools.partial(attention_kernel, shards, replicas, tile...  14.2 us
    ppermute x9, starting transfers between devices, to_replica(): return lax.ppermute(x, 'tm', pairs)  3.58 us
    ppermute x9, waiting for transfers between devices, to_replica(): return lax.ppermute(x, 'tm', pairs)  2.92 us
    pallas_call x1, Pallas kernels, per_device(): pl.pallas_call(functools.partial(pack_kernel, shards, cols), out_shape=[s...  2.21 us
  transfers between devices with their start and end apart: 26, of which 13 were waited for; matrix products, arithmetic and copies ran while one was open for 0% of the time, Pallas kernels for 0%

profile of v3, /device:TPU:0, one launch (start us, length us, event | category | flops | bytes accessed | tf_op | source)
XLA Modules:
  0.0 94.9 jit_solution(5929118748974297330)
XLA Ops:
  0.8 2.2 %pack.1 = (bf16[4,128,384]{2,1,0:T(8,128)(2,1)S(1)}, bf16[4,128,384]{2,1,0:T(8,128)(2,1)S(1)}, bf16[4,128,384]{2,1,0:T(8,128)(2,1)S(1)}, bf16[4,128,384]{2,1,0:T...) custom-call(s32[3]{0:T(128)S(1)} %pad_add_fusion.pos_ref.refs_0_, ...), custom_call_target="tpu_custom_call" | custom-call | tf_op jit(solution)/shard_map/pack/pallas_call | solution.py:273
  3.0 5.1 %collective-permute-start.7 = (bf16[2,128,384]{2,1,0:T(8,128)(2,1)S(1)}, bf16[2,128,384]{2,1,0:T(8,128)(2,1)S(1)}, u32[]{:S(2)}, u32[]{:S(2)}) collective-permute-start(bf16[2,128,384]{2,1,0:T(8,128)(2,1)S(1)} %get-tuple-element.30), channel_id=1, source_target_pairs={{0,3},{1,0},{2,1},{3,2},{4,7},{5,4},{6,5},{7,6},{8,11},{9,8},{10,9... | collective-permute-start | bytes 589832 | tf_op jit(solution)/shard_map/ppermute | solution.py:267
  10.9 1.9 %collective-permute-start = (bf16[4,128,384]{2,1,0:T(8,128)(2,1)S(1)}, bf16[4,128,384]{2,1,0:T(8,128)(2,1)S(1)}, u32[]{:S(2)}, u32[]{:S(2)}) collective-permute-start(bf16[4,128,384]{2,1,0:T(8,128)(2,1)S(1)} %get-tuple-element.27), channel_id=1, source_target_pairs={{0,8},{1,9},{2,10},{3,11},{4,12},{5,13},{6,14},{7,15},{8,0},{9,1},... | collective-permute-start | bytes 1179656 | tf_op jit(solution)/shard_map/ppermute | solution.py:267
  14.9 2.7 %collective-permute-done.8.refs_14_ = bf16[2,128,384]{2,1,0:T(8,128)(2,1)S(1)} collective-permute-done((bf16[2,128,384]{2,1,0:T(8,128)(2,1)S(1)}, bf16[2,128,384]{2,1,0:T(8,128)(2,1)S(1)}, u32[]{:S(2)}, u32[]{:S(2)}) %collective-permute-start.8) | collective-permute-done | bytes 196640 | tf_op jit(solution)/shard_map/ppermute | solution.py:267
  17.6 2.4 %collective-permute-start.2 = (bf16[4,128,384]{2,1,0:T(8,128)(2,1)S(1)}, bf16[4,128,384]{2,1,0:T(8,128)(2,1)S(1)}, u32[]{:S(2)}, u32[]{:S(2)}) collective-permute-start(bf16[4,128,384]{2,1,0:T(8,128)(2,1)S(1)} %get-tuple-element.29), channel_id=1, source_target_pairs={{0,24},{1,25},{2,26},{3,27},{4,28},{5,29},{6,30},{7,31},{8,16},{9,... | collective-permute-start | bytes 1179656 | tf_op jit(solution)/shard_map/ppermute | solution.py:267
  20.1 2.1 %collective-permute-done.9.refs_15_ = bf16[2,128,384]{2,1,0:T(8,128)(2,1)S(1)} collective-permute-done((bf16[2,128,384]{2,1,0:T(8,128)(2,1)S(1)}, bf16[2,128,384]{2,1,0:T(8,128)(2,1)S(1)}, u32[]{:S(2)}, u32[]{:S(2)}) %collective-permute-start.9) | collective-permute-done | bytes 196640 | tf_op jit(solution)/shard_map/ppermute | solution.py:267
  22.1 3.8 %collective-permute-done.10.refs_16_ = bf16[2,128,384]{2,1,0:T(8,128)(2,1)S(1)} collective-permute-done((bf16[2,128,384]{2,1,0:T(8,128)(2,1)S(1)}, bf16[2,128,384]{2,1,0:T(8,128)(2,1)S(1)}, u32[]{:S(2)}, u32[]{:S(2)}) %collective-permute-start.10) | collective-permute-done | bytes 196640 | tf_op jit(solution)/shard_map/ppermute | solution.py:267
  27.5 1.5 %collective-permute-done.refs_6_ = bf16[4,128,384]{2,1,0:T(8,128)(2,1)S(1)} collective-permute-done((bf16[4,128,384]{2,1,0:T(8,128)(2,1)S(1)}, bf16[4,128,384]{2,1,0:T(8,128)(2,1)S(1)}, u32[]{:S(2)}, u32[]{:S(2)}) %collective-permute-start) | collective-permute-done | bytes 393248 | tf_op jit(solution)/shard_map/ppermute | solution.py:267
  29.0 10.1 %collective-permute-done.1.refs_7_ = bf16[4,128,384]{2,1,0:T(8,128)(2,1)S(1)} collective-permute-done((bf16[4,128,384]{2,1,0:T(8,128)(2,1)S(1)}, bf16[4,128,384]{2,1,0:T(8,128)(2,1)S(1)}, u32[]{:S(2)}, u32[]{:S(2)}) %collective-permute-start.1) | collective-permute-done | bytes 393248 | tf_op jit(solution)/shard_map/ppermute | solution.py:267
  39.7 2.0 %collective-permute-done.14.refs_20_ = bf16[2,128,384]{2,1,0:T(8,128)(2,1)S(1)} collective-permute-done((bf16[2,128,384]{2,1,0:T(8,128)(2,1)S(1)}, bf16[2,128,384]{2,1,0:T(8,128)(2,1)S(1)}, u32[]{:S(2)}, u32[]{:S(2)}) %collective-permute-start.14) | collective-permute-done | bytes 196640 | tf_op jit(solution)/shard_map/ppermute | solution.py:271
  41.7 14.2 %attention.1 = (bf16[2,128,384]{2,1,0:T(8,128)(2,1)S(1)}, bf16[2,128,384]{2,1,0:T(8,128)(2,1)S(1)}, bf16[2,128,384]{2,1,0:T(8,128)(2,1)S(1)}, bf16[2,128,384]{2,...) custom-call(s32[3]{0:T(128)S(1)} %pad_add_fusion.pos_ref.refs_0_, ...), custom_call_target="tpu_custom_call" | custom-call | tf_op jit(solution)/shard_map/attention/pallas_call | solution.py:217
  55.9 2.3 %collective-permute-start.18 = (bf16[4,4,128,384]{3,2,1,0:T(8,128)(2,1)S(1)}, bf16[4,4,128,384]{3,2,1,0:T(8,128)(2,1)S(1)}, u32[]{:S(2)}, u32[]{:S(2)}) collective-permute-start(bf16[4,4,128,384]{3,2,1,0:T(8,128)(2,1)S(1)} %get-tuple-element.39), channel_id=1, source_target_pairs={{0,4},{4,0},{8,12},{12,8},{16,20},{20,16},{24,28},{28,24},{1,5},{5... | collective-permute-start | bytes 4718600 | tf_op jit(solution)/shard_map/ppermute | solution.py:271
  59.7 1.5 %collective-permute-start.16 = (bf16[2,128,384]{2,1,0:T(8,128)(2,1)S(1)}, bf16[2,128,384]{2,1,0:T(8,128)(2,1)S(1)}, u32[]{:S(2)}, u32[]{:S(2)}) collective-permute-start(bf16[2,128,384]{2,1,0:T(8,128)(2,1)S(1)} %get-tuple-element.36), channel_id=1, source_target_pairs={{0,16},{1,17},{2,18},{3,19},{4,20},{5,21},{6,22},{7,23},{8,24},{9,... | collective-permute-start | bytes 589832 | tf_op jit(solution)/shard_map/ppermute | solution.py:267
  62.1 1.5 %collective-permute-start.19 = (bf16[2,128,384]{2,1,0:T(8,128)(2,1)S(1)}, bf16[2,128,384]{2,1,0:T(8,128)(2,1)S(1)}, u32[]{:S(2)}, u32[]{:S(2)}) collective-permute-start(bf16[2,128,384]{2,1,0:T(8,128)(2,1)S(1)} %get-tuple-element.41), channel_id=1, source_target_pairs={{0,8},{1,9},{2,10},{3,11},{4,12},{5,13},{6,14},{7,15},{8,0},{9,1},... | collective-permute-start | bytes 589832 | tf_op jit(solution)/shard_map/ppermute | solution.py:267
  63.7 1.5 %collective-permute-start.20 = (bf16[2,128,384]{2,1,0:T(8,128)(2,1)S(1)}, bf16[2,128,384]{2,1,0:T(8,128)(2,1)S(1)}, u32[]{:S(2)}, u32[]{:S(2)}) collective-permute-start(bf16[2,128,384]{2,1,0:T(8,128)(2,1)S(1)} %get-tuple-element.42), channel_id=1, source_target_pairs={{0,16},{1,17},{2,18},{3,19},{4,20},{5,21},{6,22},{7,23},{8,24},{9,... | collective-permute-start | bytes 589832 | tf_op jit(solution)/shard_map/ppermute | solution.py:267
  66.0 2.5 %collective-permute-start.21 = (bf16[2,128,384]{2,1,0:T(8,128)(2,1)S(1)}, bf16[2,128,384]{2,1,0:T(8,128)(2,1)S(1)}, u32[]{:S(2)}, u32[]{:S(2)}) collective-permute-start(bf16[2,128,384]{2,1,0:T(8,128)(2,1)S(1)} %get-tuple-element.43), channel_id=1, source_target_pairs={{0,24},{1,25},{2,26},{3,27},{4,28},{5,29},{6,30},{7,31},{8,16},{9,... | collective-permute-start | bytes 589832 | tf_op jit(solution)/shard_map/ppermute | solution.py:267
  68.5 2.8 %collective-permute-done.16.refs_2_ = bf16[2,128,384]{2,1,0:T(8,128)(2,1)S(1)} collective-permute-done((bf16[2,128,384]{2,1,0:T(8,128)(2,1)S(1)}, bf16[2,128,384]{2,1,0:T(8,128)(2,1)S(1)}, u32[]{:S(2)}, u32[]{:S(2)}) %collective-permute-start.16) | collective-permute-done | bytes 196640 | tf_op jit(solution)/shard_map/ppermute | solution.py:267
  71.3 5.4 %collective-permute-start.23 = (bf16[2,128,384]{2,1,0:T(8,128)(2,1)S(1)}, bf16[2,128,384]{2,1,0:T(8,128)(2,1)S(1)}, u32[]{:S(2)}, u32[]{:S(2)}) collective-permute-start(bf16[2,128,384]{2,1,0:T(8,128)(2,1)S(1)} %get-tuple-element.45), channel_id=1, source_target_pairs={{0,9},{1,10},{2,11},{3,8},{4,13},{5,14},{6,15},{7,12},{8,1},{9,2},... | collective-permute-start | bytes 589832 | tf_op jit(solution)/shard_map/ppermute | solution.py:267
  76.6 3.0 %collective-permute-start.24 = (bf16[2,128,384]{2,1,0:T(8,128)(2,1)S(1)}, bf16[2,128,384]{2,1,0:T(8,128)(2,1)S(1)}, u32[]{:S(2)}, u32[]{:S(2)}) collective-permute-start(bf16[2,128,384]{2,1,0:T(8,128)(2,1)S(1)} %get-tuple-element.46), channel_id=1, source_target_pairs={{0,17},{1,18},{2,19},{3,16},{4,21},{5,22},{6,23},{7,20},{8,25},{9,... | collective-permute-start | bytes 589832 | tf_op jit(solution)/shard_map/ppermute | solution.py:267
  79.6 2.8 %collective-permute-start.25 = (bf16[2,128,384]{2,1,0:T(8,128)(2,1)S(1)}, bf16[2,128,384]{2,1,0:T(8,128)(2,1)S(1)}, u32[]{:S(2)}, u32[]{:S(2)}) collective-permute-start(bf16[2,128,384]{2,1,0:T(8,128)(2,1)S(1)} %get-tuple-element.47), channel_id=1, source_target_pairs={{0,25},{1,26},{2,27},{3,24},{4,29},{5,30},{6,31},{7,28},{8,17},{9,... | collective-permute-start | bytes 589832 | tf_op jit(solution)/shard_map/ppermute | solution.py:267
  82.4 3.7 %collective-permute-done.23.refs_9_ = bf16[2,128,384]{2,1,0:T(8,128)(2,1)S(1)} collective-permute-done((bf16[2,128,384]{2,1,0:T(8,128)(2,1)S(1)}, bf16[2,128,384]{2,1,0:T(8,128)(2,1)S(1)}, u32[]{:S(2)}, u32[]{:S(2)}) %collective-permute-start.23) | collective-permute-done | bytes 196640 | tf_op jit(solution)/shard_map/ppermute | solution.py:267
  86.2 4.8 %collective-permute-done.24.refs_10_ = bf16[2,128,384]{2,1,0:T(8,128)(2,1)S(1)} collective-permute-done((bf16[2,128,384]{2,1,0:T(8,128)(2,1)S(1)}, bf16[2,128,384]{2,1,0:T(8,128)(2,1)S(1)}, u32[]{:S(2)}, u32[]{:S(2)}) %collective-permute-start.24) | collective-permute-done | bytes 196640 | tf_op jit(solution)/shard_map/ppermute | solution.py:267
  91.0 2.1 %collective-permute-done.25.refs_11_ = bf16[2,128,384]{2,1,0:T(8,128)(2,1)S(1)} collective-permute-done((bf16[2,128,384]{2,1,0:T(8,128)(2,1)S(1)}, bf16[2,128,384]{2,1,0:T(8,128)(2,1)S(1)}, u32[]{:S(2)}, u32[]{:S(2)}) %collective-permute-start.25) | collective-permute-done | bytes 196640 | tf_op jit(solution)/shard_map/ppermute | solution.py:267
  93.1 1.8 %unpack.1 = (bf16[128,1536]{1,0:T(8,128)(2,1)}, bf16[128,1536]{1,0:T(8,128)(2,1)}, bf16[128,1536]{1,0:T(8,128)(2,1)}, bf16[128,1536]{1,0:T(8,128)(2,1)}) custom-call(s32[3]{0:T(128)S(1)} %pad_add_fusion.pos_ref.refs_0_, bf16[2,128,384]{2,1,0:T(8,128)(2,1)S(1)} %get-tuple-element.34.refs_0_, bf16[2,128,384]{2,1,0:T(8,128)(2,1)S(1)} %collective-permute-done.15.refs_1_, ...), custom_call_target="tpu_custom_call" | custom-call | tf_op jit(solution)/shard_map/unpack/pallas_call | solution.py:308
  (41 shorter events, 10.4 us)
Async XLA Ops:
  3.0 10.4 %collective-permute-start.7 = (bf16[2,128,384]{2,1,0:T(8,128)(2,1)S(1)}, bf16[2,128,384]{2,1,0:T(8,128)(2,1)S(1)}, u32[]{:S(2)}, u32[]{:S(2)}) collective-permute-start(bf16[2,128,384]{2,1,0:T(8,128)(2,1)S(1)} %get-tuple-element.30), channel_id=1, source_target_pairs={{0,3},{1,0},{2,1},{3,2},{4,7},{5,4},{6,5},{7,6},{8,11},{9,8},{10,9... | collective-permute-start | bytes 589832 | tf_op jit(solution)/shard_map/ppermute | solution.py:267
  8.1 9.5 %collective-permute-start.8 = (bf16[2,128,384]{2,1,0:T(8,128)(2,1)S(1)}, bf16[2,128,384]{2,1,0:T(8,128)(2,1)S(1)}, u32[]{:S(2)}, u32[]{:S(2)}) collective-permute-start(bf16[2,128,384]{2,1,0:T(8,128)(2,1)S(1)} %get-tuple-element.31), channel_id=1, source_target_pairs={{0,11},{1,8},{2,9},{3,10},{4,15},{5,12},{6,13},{7,14},{8,3},{9,0},... | collective-permute-start | bytes 589832 | tf_op jit(solution)/shard_map/ppermute | solution.py:267
  9.5 12.6 %collective-permute-start.9 = (bf16[2,128,384]{2,1,0:T(8,128)(2,1)S(1)}, bf16[2,128,384]{2,1,0:T(8,128)(2,1)S(1)}, u32[]{:S(2)}, u32[]{:S(2)}) collective-permute-start(bf16[2,128,384]{2,1,0:T(8,128)(2,1)S(1)} %get-tuple-element.32), channel_id=1, source_target_pairs={{0,19},{1,16},{2,17},{3,18},{4,23},{5,20},{6,21},{7,22},{8,27},{9,... | collective-permute-start | bytes 589832 | tf_op jit(solution)/shard_map/ppermute | solution.py:267
  10.9 15.0 %collective-permute-start.10 = (bf16[2,128,384]{2,1,0:T(8,128)(2,1)S(1)}, bf16[2,128,384]{2,1,0:T(8,128)(2,1)S(1)}, u32[]{:S(2)}, u32[]{:S(2)}) collective-permute-start(bf16[2,128,384]{2,1,0:T(8,128)(2,1)S(1)} %get-tuple-element.33), channel_id=1, source_target_pairs={{0,27},{1,24},{2,25},{3,26},{4,31},{5,28},{6,29},{7,30},{8,19},{9,... | collective-permute-start | bytes 589832 | tf_op jit(solution)/shard_map/ppermute | solution.py:267
  10.9 18.1 %collective-permute-start = (bf16[4,128,384]{2,1,0:T(8,128)(2,1)S(1)}, bf16[4,128,384]{2,1,0:T(8,128)(2,1)S(1)}, u32[]{:S(2)}, u32[]{:S(2)}) collective-permute-start(bf16[4,128,384]{2,1,0:T(8,128)(2,1)S(1)} %get-tuple-element.27), channel_id=1, source_target_pairs={{0,8},{1,9},{2,10},{3,11},{4,12},{5,13},{6,14},{7,15},{8,0},{9,1},... | collective-permute-start | bytes 1179656 | tf_op jit(solution)/shard_map/ppermute | solution.py:267
  13.4 25.7 %collective-permute-start.1 = (bf16[4,128,384]{2,1,0:T(8,128)(2,1)S(1)}, bf16[4,128,384]{2,1,0:T(8,128)(2,1)S(1)}, u32[]{:S(2)}, u32[]{:S(2)}) collective-permute-start(bf16[4,128,384]{2,1,0:T(8,128)(2,1)S(1)} %get-tuple-element.28), channel_id=1, source_target_pairs={{0,16},{1,17},{2,18},{3,19},{4,20},{5,21},{6,22},{7,23},{8,24},{9,... | collective-permute-start | bytes 1179656 | tf_op jit(solution)/shard_map/ppermute | solution.py:267
  17.6 21.5 %collective-permute-start.2 = (bf16[4,128,384]{2,1,0:T(8,128)(2,1)S(1)}, bf16[4,128,384]{2,1,0:T(8,128)(2,1)S(1)}, u32[]{:S(2)}, u32[]{:S(2)}) collective-permute-start(bf16[4,128,384]{2,1,0:T(8,128)(2,1)S(1)} %get-tuple-element.29), channel_id=1, source_target_pairs={{0,24},{1,25},{2,26},{3,27},{4,28},{5,29},{6,30},{7,31},{8,16},{9,... | collective-permute-start | bytes 1179656 | tf_op jit(solution)/shard_map/ppermute | solution.py:267
  22.1 3.8 %collective-permute-start.11 = (bf16[2,128,384]{2,1,0:T(8,128)(2,1)S(1)}, bf16[2,128,384]{2,1,0:T(8,128)(2,1)S(1)}, u32[]{:S(2)}, u32[]{:S(2)}) collective-permute-start(bf16[2,128,384]{2,1,0:T(8,128)(2,1)S(1)} %collective-permute-done.7.refs_13_), channel_id=1, source_target_pairs={{0,4},{4,0},{8,12},{12,8},{16,20},{20,16},{24,28},{28,24},{1,5},{5... | collective-permute-start | bytes 589832 | tf_op jit(solution)/shard_map/ppermute | solution.py:271
  25.9 15.8 %collective-permute-start.3 = (bf16[4,128,384]{2,1,0:T(8,128)(2,1)S(1)}, bf16[4,128,384]{2,1,0:T(8,128)(2,1)S(1)}, u32[]{:S(2)}, u32[]{:S(2)}) collective-permute-start(bf16[4,128,384]{2,1,0:T(8,128)(2,1)S(1)} %get-tuple-element.26.refs_5_), channel_id=1, source_target_pairs={{0,4},{4,0},{8,12},{12,8},{16,20},{20,16},{24,28},{28,24},{1,5},{5... | collective-permute-start | bytes 1179656 | tf_op jit(solution)/shard_map/ppermute | solution.py:271
  27.3 12.3 %collective-permute-start.13 = (bf16[2,128,384]{2,1,0:T(8,128)(2,1)S(1)}, bf16[2,128,384]{2,1,0:T(8,128)(2,1)S(1)}, u32[]{:S(2)}, u32[]{:S(2)}) collective-permute-start(bf16[2,128,384]{2,1,0:T(8,128)(2,1)S(1)} %collective-permute-done.9.refs_15_), channel_id=1, source_target_pairs={{0,4},{4,0},{8,12},{12,8},{16,20},{20,16},{24,28},{28,24},{1,5},{5... | collective-permute-start | bytes 589832 | tf_op jit(solution)/shard_map/ppermute | solution.py:271
  29.0 12.7 %collective-permute-start.4 = (bf16[4,128,384]{2,1,0:T(8,128)(2,1)S(1)}, bf16[4,128,384]{2,1,0:T(8,128)(2,1)S(1)}, u32[]{:S(2)}, u32[]{:S(2)}) collective-permute-start(bf16[4,128,384]{2,1,0:T(8,128)(2,1)S(1)} %collective-permute-done.refs_6_), channel_id=1, source_target_pairs={{0,4},{4,0},{8,12},{12,8},{16,20},{20,16},{24,28},{28,24},{1,5},{5... | collective-permute-start | bytes 1179656 | tf_op jit(solution)/shard_map/ppermute | solution.py:271
  39.1 2.6 %collective-permute-start.5 = (bf16[4,128,384]{2,1,0:T(8,128)(2,1)S(1)}, bf16[4,128,384]{2,1,0:T(8,128)(2,1)S(1)}, u32[]{:S(2)}, u32[]{:S(2)}) collective-permute-start(bf16[4,128,384]{2,1,0:T(8,128)(2,1)S(1)} %collective-permute-done.1.refs_7_), channel_id=1, source_target_pairs={{0,4},{4,0},{8,12},{12,8},{16,20},{20,16},{24,28},{28,24},{1,5},{5... | collective-permute-start | bytes 1179656 | tf_op jit(solution)/shard_map/ppermute | solution.py:271
  39.1 2.6 %collective-permute-start.6 = (bf16[4,128,384]{2,1,0:T(8,128)(2,1)S(1)}, bf16[4,128,384]{2,1,0:T(8,128)(2,1)S(1)}, u32[]{:S(2)}, u32[]{:S(2)}) collective-permute-start(bf16[4,128,384]{2,1,0:T(8,128)(2,1)S(1)} %collective-permute-done.2.refs_8_), channel_id=1, source_target_pairs={{0,4},{4,0},{8,12},{12,8},{16,20},{20,16},{24,28},{28,24},{1,5},{5... | collective-permute-start | bytes 1179656 | tf_op jit(solution)/shard_map/ppermute | solution.py:271
  55.9 5.8 %collective-permute-start.18 = (bf16[4,4,128,384]{3,2,1,0:T(8,128)(2,1)S(1)}, bf16[4,4,128,384]{3,2,1,0:T(8,128)(2,1)S(1)}, u32[]{:S(2)}, u32[]{:S(2)}) collective-permute-start(bf16[4,4,128,384]{3,2,1,0:T(8,128)(2,1)S(1)} %get-tuple-element.39), channel_id=1, source_target_pairs={{0,4},{4,0},{8,12},{12,8},{16,20},{20,16},{24,28},{28,24},{1,5},{5... | collective-permute-start | bytes 4718600 | tf_op jit(solution)/shard_map/ppermute | solution.py:271
  58.2 7.8 %collective-permute-start.15 = (bf16[2,128,384]{2,1,0:T(8,128)(2,1)S(1)}, bf16[2,128,384]{2,1,0:T(8,128)(2,1)S(1)}, u32[]{:S(2)}, u32[]{:S(2)}) collective-permute-start(bf16[2,128,384]{2,1,0:T(8,128)(2,1)S(1)} %get-tuple-element.35), channel_id=1, source_target_pairs={{0,8},{1,9},{2,10},{3,11},{4,12},{5,13},{6,14},{7,15},{8,0},{9,1},... | collective-permute-start | bytes 589832 | tf_op jit(solution)/shard_map/ppermute | solution.py:267
  59.7 11.5 %collective-permute-start.16 = (bf16[2,128,384]{2,1,0:T(8,128)(2,1)S(1)}, bf16[2,128,384]{2,1,0:T(8,128)(2,1)S(1)}, u32[]{:S(2)}, u32[]{:S(2)}) collective-permute-start(bf16[2,128,384]{2,1,0:T(8,128)(2,1)S(1)} %get-tuple-element.36), channel_id=1, source_target_pairs={{0,16},{1,17},{2,18},{3,19},{4,20},{5,21},{6,22},{7,23},{8,24},{9,... | collective-permute-start | bytes 589832 | tf_op jit(solution)/shard_map/ppermute | solution.py:267
  61.3 10.0 %collective-permute-start.17 = (bf16[2,128,384]{2,1,0:T(8,128)(2,1)S(1)}, bf16[2,128,384]{2,1,0:T(8,128)(2,1)S(1)}, u32[]{:S(2)}, u32[]{:S(2)}) collective-permute-start(bf16[2,128,384]{2,1,0:T(8,128)(2,1)S(1)} %get-tuple-element.37), channel_id=1, source_target_pairs={{0,24},{1,25},{2,26},{3,27},{4,28},{5,29},{6,30},{7,31},{8,16},{9,... | collective-permute-start | bytes 589832 | tf_op jit(solution)/shard_map/ppermute | solution.py:267
  62.1 14.5 %collective-permute-start.19 = (bf16[2,128,384]{2,1,0:T(8,128)(2,1)S(1)}, bf16[2,128,384]{2,1,0:T(8,128)(2,1)S(1)}, u32[]{:S(2)}, u32[]{:S(2)}) collective-permute-start(bf16[2,128,384]{2,1,0:T(8,128)(2,1)S(1)} %get-tuple-element.41), channel_id=1, source_target_pairs={{0,8},{1,9},{2,10},{3,11},{4,12},{5,13},{6,14},{7,15},{8,0},{9,1},... | collective-permute-start | bytes 589832 | tf_op jit(solution)/shard_map/ppermute | solution.py:267
  63.7 15.9 %collective-permute-start.20 = (bf16[2,128,384]{2,1,0:T(8,128)(2,1)S(1)}, bf16[2,128,384]{2,1,0:T(8,128)(2,1)S(1)}, u32[]{:S(2)}, u32[]{:S(2)}) collective-permute-start(bf16[2,128,384]{2,1,0:T(8,128)(2,1)S(1)} %get-tuple-element.42), channel_id=1, source_target_pairs={{0,16},{1,17},{2,18},{3,19},{4,20},{5,21},{6,22},{7,23},{8,24},{9,... | collective-permute-start | bytes 589832 | tf_op jit(solution)/shard_map/ppermute | solution.py:267
  66.0 16.4 %collective-permute-start.21 = (bf16[2,128,384]{2,1,0:T(8,128)(2,1)S(1)}, bf16[2,128,384]{2,1,0:T(8,128)(2,1)S(1)}, u32[]{:S(2)}, u32[]{:S(2)}) collective-permute-start(bf16[2,128,384]{2,1,0:T(8,128)(2,1)S(1)} %get-tuple-element.43), channel_id=1, source_target_pairs={{0,24},{1,25},{2,26},{3,27},{4,28},{5,29},{6,30},{7,31},{8,16},{9,... | collective-permute-start | bytes 589832 | tf_op jit(solution)/shard_map/ppermute | solution.py:267
  71.3 11.2 %collective-permute-start.22 = (bf16[2,128,384]{2,1,0:T(8,128)(2,1)S(1)}, bf16[2,128,384]{2,1,0:T(8,128)(2,1)S(1)}, u32[]{:S(2)}, u32[]{:S(2)}) collective-permute-start(bf16[2,128,384]{2,1,0:T(8,128)(2,1)S(1)} %get-tuple-element.44), channel_id=1, source_target_pairs={{0,1},{1,2},{2,3},{3,0},{4,5},{5,6},{6,7},{7,4},{8,9},{9,10},{10,1... | collective-permute-start | bytes 589832 | tf_op jit(solution)/shard_map/ppermute | solution.py:267
  71.3 14.9 %collective-permute-start.23 = (bf16[2,128,384]{2,1,0:T(8,128)(2,1)S(1)}, bf16[2,128,384]{2,1,0:T(8,128)(2,1)S(1)}, u32[]{:S(2)}, u32[]{:S(2)}) collective-permute-start(bf16[2,128,384]{2,1,0:T(8,128)(2,1)S(1)} %get-tuple-element.45), channel_id=1, source_target_pairs={{0,9},{1,10},{2,11},{3,8},{4,13},{5,14},{6,15},{7,12},{8,1},{9,2},... | collective-permute-start | bytes 589832 | tf_op jit(solution)/shard_map/ppermute | solution.py:267
  76.6 14.3 %collective-permute-start.24 = (bf16[2,128,384]{2,1,0:T(8,128)(2,1)S(1)}, bf16[2,128,384]{2,1,0:T(8,128)(2,1)S(1)}, u32[]{:S(2)}, u32[]{:S(2)}) collective-permute-start(bf16[2,128,384]{2,1,0:T(8,128)(2,1)S(1)} %get-tuple-element.46), channel_id=1, source_target_pairs={{0,17},{1,18},{2,19},{3,16},{4,21},{5,22},{6,23},{7,20},{8,25},{9,... | collective-permute-start | bytes 589832 | tf_op jit(solution)/shard_map/ppermute | solution.py:267
  79.6 13.5 %collective-permute-start.25 = (bf16[2,128,384]{2,1,0:T(8,128)(2,1)S(1)}, bf16[2,128,384]{2,1,0:T(8,128)(2,1)S(1)}, u32[]{:S(2)}, u32[]{:S(2)}) collective-permute-start(bf16[2,128,384]{2,1,0:T(8,128)(2,1)S(1)} %get-tuple-element.47), channel_id=1, source_target_pairs={{0,25},{1,26},{2,27},{3,24},{4,29},{5,30},{6,31},{7,28},{8,17},{9,... | collective-permute-start | bytes 589832 | tf_op jit(solution)/shard_map/ppermute | solution.py:267
  (6 other events, 167.7 us)
